TPU v7x, 32 devices: a whole 2x2x4 slice. The times are simulated.
32 devices in a mesh: groups: 2 (over y), seq: 4 (over z), tensor: 2 (over x), sub: 2 (over core).
Axes of the slice: x: 2, y: 2, z: 4, core: 2. Of those that a mesh axis runs over, the one named last changes fastest.
Arguments:
- query: bfloat16 [2048, 32, 128], P(('groups', 'seq'), ('tensor', 'sub')), parts along dimension 0, may hold values from -24 to 24
- key_states: bfloat16 [2048, 8, 128], P(('groups', 'seq'), 'tensor'), parts along dimension 0, may hold values from -8.4 to 8.4
- value_states: bfloat16 [2048, 8, 128], P(('groups', 'seq'), 'tensor'), parts along dimension 0, may hold values from -16 to 16
- grad_out: bfloat16 [2048, 32, 128], P(('groups', 'seq'), ('tensor', 'sub')), parts along dimension 0, may hold values from -6 to 6
- block_mask: int32 [16, 17], P(('groups', 'seq')), parts along dimension 0, may hold values from 0 to 1, as said below
Outputs:
- attended: bfloat16 [2048, 32, 128], P(('groups', 'seq'), ('tensor', 'sub')), parts along dimension 0
- query_grad: bfloat16 [2048, 32, 128], P(('groups', 'seq'), ('tensor', 'sub')), parts along dimension 0
- key_grad: bfloat16 [2048, 8, 128], P(('groups', 'seq'), 'tensor'), parts along dimension 0
- value_grad: bfloat16 [2048, 8, 128], P(('groups', 'seq'), 'tensor'), parts along dimension 0
There are 2 independent parts, one for each index of `groups`. A program takes and returns all parts, laid end to end along the dimension named above; each array names one. Nothing has to cross between parts.
Inputs may be any that keep to these rules, and one draw needn't show every extreme that they name: `block_mask`: entries are 0 or 1; entry 0 of every row is 1.
All inputs are finite; a program needn't handle non-finite values.
Results may differ from a plain program's by a relative error of at most 0.012.
The roundings to bfloat16 on the way count: a program that leaves them out, or rounds other values in their place, can miss the bound.
Values may be sent and summed in bfloat16 or wider, within the bound.
No kernel may reach another device: no remote copies, remote signals or barrier semaphores. Data moves between devices by JAX's collectives and lax.ppermute only.
A program may use at most 64 MiB of HBM per device.

v0:
```python
import math

import jax
import jax.numpy as jnp
from jax import lax
from jax.sharding import PartitionSpec as P

HEADS = 32
KV_HEADS = 8
BLOCK = 128
WINDOW = 2048


NEGATIVE = -1e30


def from_behind(value, axis, steps):
    count = lax.axis_size(axis)
    first, last = (max(0, -steps), min(count, count - steps))
    return lax.ppermute(value, axis, [(source, source + steps) for source in range(first, last)])


def body(query, key_states, value_states, grad_out, block_mask):
    row_count, q_heads, head_size = query.shape
    kv_heads = key_states.shape[1]
    score_scale = 1.0 / math.sqrt(head_size)
    block_count = row_count // BLOCK
    offset_count = block_mask.shape[1]
    hop_count = min(WINDOW // row_count, lax.axis_size("seq") - 1)
    shard_index = lax.axis_index("seq")
    core_index = lax.axis_index("sub")
    group_size = HEADS // KV_HEADS
    kv_index = (core_index * q_heads + jnp.arange(q_heads, dtype=jnp.int32)) // group_size
    chosen = kv_index[:, None] == jnp.arange(kv_heads, dtype=jnp.int32)[None, :]
    pick_low = chosen.astype(jnp.bfloat16)
    pick_wide = chosen.astype(jnp.float32)

    def widen(states):
        return jnp.sum(states[:, None, :, :] * pick_low[None, :, :, None], axis=2)

    def narrow(terms):
        return jnp.sum(terms[:, :, None, :] * pick_wide[None, :, :, None], axis=1)

    kv_pair = jnp.stack((key_states, value_states), 0)
    arrived = []
    moving = kv_pair
    for step_number in range(hop_count):
        moving = from_behind(moving, "seq", 1)
        arrived.append(moving)
    remote = jnp.stack(arrived[::-1], 0)
    stacked = jnp.concatenate([remote, kv_pair[None]], 0)
    slot_numbers = jnp.arange(hop_count + 1, dtype=jnp.int32)
    query_pos = jnp.arange(row_count, dtype=jnp.int32)

    def tile_allowed(slot_index):
        lag_shards = hop_count - slot_index
        query_block = jnp.arange(block_count, dtype=jnp.int32)[:, None, None]
        key_block = jnp.arange(block_count, dtype=jnp.int32)[None, :, None]
        offset_axis = jnp.arange(offset_count, dtype=jnp.int32)[None, None, :]
        hit = offset_axis == query_block + lag_shards * block_count - key_block
        coarse = jnp.sum(jnp.where(hit, block_mask[:, None, :], 0), axis=2) > 0
        token_mask = jnp.repeat(jnp.repeat(coarse, BLOCK, axis=0), BLOCK, axis=1)
        token_gap = query_pos[:, None] + lag_shards * row_count - query_pos[None, :]
        return (
            token_mask & (token_gap >= 0) & (token_gap < WINDOW) & (shard_index - lag_shards >= 0)
        )

    def masked_scores(slot_index, key_tile):
        raw_scores = (
            jnp.einsum("qhd,khd->hqk", query, key_tile, preferred_element_type=jnp.float32)
            * score_scale
        )
        return jnp.where(tile_allowed(slot_index)[None], raw_scores, NEGATIVE)

    def gather_stats(carry, inputs):
        row_max, row_sum = carry
        slot_index, pair_now = inputs
        masked = masked_scores(slot_index, widen(pair_now[0]))
        new_max = jnp.maximum(row_max, jnp.max(masked, axis=2))
        row_sum = row_sum * jnp.exp(row_max - new_max) + jnp.sum(
            jnp.exp(masked - new_max[:, :, None]), axis=2
        )
        return ((new_max, row_sum), None)

    start_stats = (
        jnp.full((q_heads, row_count), NEGATIVE, jnp.float32),
        jnp.zeros((q_heads, row_count), jnp.float32),
    )
    (row_max, row_sum), unused = lax.scan(gather_stats, start_stats, (slot_numbers, stacked))
    log_total = row_max + jnp.log(row_sum)

    def add_values(accum, inputs):
        slot_index, pair_now = inputs
        masked = masked_scores(slot_index, widen(pair_now[0]))
        weights = jnp.exp(masked - log_total[:, :, None]).astype(jnp.bfloat16)
        return (
            accum
            + jnp.einsum(
                "hqk,khd->qhd", weights, widen(pair_now[1]), preferred_element_type=jnp.float32
            ),
            None,
        )

    zero_rows = jnp.zeros((row_count, q_heads, head_size), jnp.float32)
    accum, unused = lax.scan(add_values, zero_rows, (slot_numbers, stacked))
    attended = accum.astype(jnp.bfloat16)
    drift = jnp.sum(grad_out.astype(jnp.float32) * attended.astype(jnp.float32), axis=2).T

    def backward_tile(accum, inputs):
        slot_index, pair_now = inputs
        key_tile = widen(pair_now[0])
        value_tile = widen(pair_now[1])
        exact = jnp.exp(masked_scores(slot_index, key_tile) - log_total[:, :, None])
        weights = exact.astype(jnp.bfloat16)
        value_part = narrow(
            jnp.einsum("hqk,qhd->khd", weights, grad_out, preferred_element_type=jnp.float32)
        )
        pushed = jnp.einsum(
            "qhd,khd->hqk", grad_out, value_tile, preferred_element_type=jnp.float32
        )
        slope = (exact * (pushed - drift[:, :, None])).astype(jnp.bfloat16)
        accum = (
            accum
            + jnp.einsum("hqk,khd->qhd", slope, key_tile, preferred_element_type=jnp.float32)
            * score_scale
        )
        key_part = narrow(
            jnp.einsum("hqk,qhd->khd", slope, query, preferred_element_type=jnp.float32)
            * score_scale
        )
        return (accum, jnp.stack((key_part, value_part), 0))

    query_accum, partials = lax.scan(backward_tile, zero_rows, (slot_numbers, stacked))
    query_grad = query_accum.astype(jnp.bfloat16)
    flat_terms = partials.reshape(hop_count + 1, 2, row_count, kv_heads * head_size)
    moving = flat_terms[0]
    for slot_index in range(1, hop_count + 1):
        moving = from_behind(moving, "seq", -1) + flat_terms[slot_index]
    summed = lax.psum(moving.astype(jnp.bfloat16), "sub")
    key_grad = summed[0].reshape(row_count, kv_heads, head_size)
    value_grad = summed[1].reshape(row_count, kv_heads, head_size)
    return (attended, query_grad, key_grad, value_grad)


def solution(mesh):
    in_specs = (
        P(("groups", "seq"), ("tensor", "sub"), None),
        P(("groups", "seq"), "tensor", None),
        P(("groups", "seq"), "tensor", None),
        P(("groups", "seq"), ("tensor", "sub"), None),
        P(("groups", "seq"), None),
    )
    out_specs = (
        P(("groups", "seq"), ("tensor", "sub"), None),
        P(("groups", "seq"), ("tensor", "sub"), None),
        P(("groups", "seq"), "tensor", None),
        P(("groups", "seq"), "tensor", None),
    )
    return jax.shard_map(body, mesh=mesh, in_specs=in_specs, out_specs=out_specs, check_vma=False)
```

profile of v0, /device:TPU:13, one launch (start us, length us, event | category | flops | bytes accessed | tf_op | source)
XLA Modules:
  0.0 276.1 jit_solution(17757706338250342390)
XLA Ops:
  7.2 2.3 pad_maximum_fusion.1
  9.5 3.2 %collective-permute-start = (bf16[2,256,4,128]{3,2,1,0:T(4,128)(2,1)S(1)}, bf16[2,256,4,128]{3,2,1,0:T(4,128)(2,1)S(1)}, u32[]{:S(2)}, u32[]{:S(2)}) collective-permute-start(bf16[2,256,4,128]{3,2,1,0:T(4,128)(2,1)S(1)} %get-tuple-element.945), channel_id=1, source_target_pairs={{0,4},{4,8},{8,12},{1,5},{5,9},{9,13},{2,6},{6,10},{10,14},{3,7},{... | collective-permute-start | bytes 1572872 | tf_op jit(solution)/shard_map/ppermute | solution.py:20
  12.7 11.5 %collective-permute-done = bf16[2,256,4,128]{3,2,1,0:T(4,128)(2,1)S(1)} collective-permute-done((bf16[2,256,4,128]{3,2,1,0:T(4,128)(2,1)S(1)}, bf16[2,256,4,128]{3,2,1,0:T(4,128)(2,1)S(1)}, u32[]{:S(2)}, u32[]{:S(2)}) %collective-permute-start) | collective-permute-done | bytes 524320 | tf_op jit(solution)/shard_map/ppermute | solution.py:20
  24.2 3.2 %collective-permute-start.1 = (bf16[2,256,4,128]{3,2,1,0:T(4,128)(2,1)S(1)}, bf16[2,256,4,128]{3,2,1,0:T(4,128)(2,1)S(1)}, u32[]{:S(2)}, u32[]{:S(2)}) collective-permute-start(bf16[2,256,4,128]{3,2,1,0:T(4,128)(2,1)S(1)} %collective-permute-done), channel_id=1, source_target_pairs={{0,4},{4,8},{8,12},{1,5},{5,9},{9,13},{2,6},{6,10},{10,14},{3,7},{... | collective-permute-start | bytes 1572872 | tf_op jit(solution)/shard_map/ppermute | solution.py:20
  27.4 10.6 %collective-permute-done.1 = bf16[2,256,4,128]{3,2,1,0:T(4,128)(2,1)S(1)} collective-permute-done((bf16[2,256,4,128]{3,2,1,0:T(4,128)(2,1)S(1)}, bf16[2,256,4,128]{3,2,1,0:T(4,128)(2,1)S(1)}, u32[]{:S(2)}, u32[]{:S(2)}) %collective-permute-start.1) | collective-permute-done | bytes 524320 | tf_op jit(solution)/shard_map/ppermute | solution.py:20
  37.9 3.2 %collective-permute-start.2 = (bf16[2,256,4,128]{3,2,1,0:T(4,128)(2,1)S(1)}, bf16[2,256,4,128]{3,2,1,0:T(4,128)(2,1)S(1)}, u32[]{:S(2)}, u32[]{:S(2)}) collective-permute-start(bf16[2,256,4,128]{3,2,1,0:T(4,128)(2,1)S(1)} %collective-permute-done.1), channel_id=1, source_target_pairs={{0,4},{4,8},{8,12},{1,5},{5,9},{9,13},{2,6},{6,10},{10,14},{3,7},{... | collective-permute-start | bytes 1572872 | tf_op jit(solution)/shard_map/ppermute | solution.py:20
  41.2 1.1 copy.54
  42.4 8.3 %collective-permute-done.2 = bf16[2,256,4,128]{3,2,1,0:T(4,128)(2,1)S(1)} collective-permute-done((bf16[2,256,4,128]{3,2,1,0:T(4,128)(2,1)S(1)}, bf16[2,256,4,128]{3,2,1,0:T(4,128)(2,1)S(1)}, u32[]{:S(2)}, u32[]{:S(2)}) %collective-permute-start.2) | collective-permute-done | bytes 524320 | tf_op jit(solution)/shard_map/ppermute | solution.py:20
  50.8 0.8 copy-done.8
  51.6 3.1 %pad_maximum_fusion = bf16[4,2,256,4,128]{4,3,2,1,0:T(4,128)(2,1)S(1)} fusion(bf16[1,2,256,4,128]{4,3,2,1,0:T(4,128)(2,1)} %get-tuple-element.946, bf16[1,2,256,4,128]{4,3,2,1,0:T(4,128)(2,1)} %bitcast.183, bf16[1,2,256,4,128]{4,3,2,1,0:T(4,128)(2,1)} %bitcast.184, bf16[1,2,256,4,128]{4,3,2,1,0:T(4,128)(2,1)} %bitcast.185), kind=kLoop, calls=%fused_computation.106 | loop fusion | flops 3145728 | bytes 4194304 | tf_op jit(solution)/shard_map/concatenate | solution.py:51
  54.8 16.5 %while.50 = (s32[]{:T(128)}, f32[8,256]{1,0:T(8,128)S(1)}, f32[8,256]{1,0:T(8,128)S(1)}, s32[4]{0:T(128)S(1)}, s32[2,17]{1,0:T(2,128)S(1)}, /*index=5*/s32[]{:T(...) while((s32[]{:T(128)}, f32[8,256]{1,0:T(8,128)S(1)}, ...), condition=%wide.region_5.6_spmd.clone.clone, body=%wide.region_0.5_spmd.clone.clone.sunk | while | flops 140126752 | bytes 6861426 | solution.py:89
  56.8 1.1 multiply_reduce_fusion.12
  60.9 1.1 multiply_reduce_fusion.12
  65.0 1.1 multiply_reduce_fusion.12
  69.1 1.1 multiply_reduce_fusion.12
  71.3 33.6 %while.51 = (s32[]{:T(128)}, f32[256,8,128]{0,2,1:T(8,128)}, bf16[4,2,256,4,128]{4,3,2,1,0:T(4,128)(2,1)S(1)}, s32[4]{0:T(128)S(1)}, s32[2,17]{1,0:T(2,128)S(1)}...) while((s32[]{:T(128)}, f32[256,8,128]{0,2,1:T(8,128)}, ...), condition=%wide.region_10.11_spmd.clone.clone, body=%wide.region_6.10_spmd.clone.clone.sunk | while | flops 275120672 | bytes 6435465 | solution.py:105
  73.4 3.0 %multiply_reduce_fusion.13 = (bf16[256,8,128]{2,1,0:T(8,128)(2,1)}, bf16[256,8,128]{2,1,0:T(8,128)(2,1)}) fusion(bf16[256,4,128]{2,1,0:T(4,128)(2,1)S(1)} %get-tuple-element.1134, bf16[8,4]{0,1:T(4,128)(2,1)S(1)} %fusion.119, bf16[256,4,128]{2,1,0:T(4,128)(2,1)S(1)} %get-tuple-element.1135), kind=kLoop, calls=%fused_computation.37.clone.1 | loop fusion | flops 3670016 | bytes 1572928 | tf_op jit(solution)/shard_map/while/body/eval_jaxpr/reduce_sum | solution.py:39
  76.4 3.1 %fusion.120 = f32[256,8,128]{0,2,1:T(8,128)} fusion(bf16[256,8,128]{2,0,1:T(8,128)(2,1)S(1)} %get-tuple-element.1236, f32[256,8,128]{0,2,1:T(8,128)} %get-tuple-element.1216, f32[8,256]{1,0:T(8,128)S(1)} %get-tuple-element.1237, pred[256,256]{0,1:T(8,128)(4,1)S(1)} %fusion.118, bf16[256,8,128]{2,1,0:T(8,128)(2,1)} %get-tuple-element.1136, ...), kind=kOutput, calls=%fused_computation.41.clone.1 | convolution fusion | flops 271056896 | bytes 3743745 | tf_op jit(solution)/shard_map/while/body/eval_jaxpr/hqk,khd->qhd/dot_general | solution.py:98
  81.5 3.0 %multiply_reduce_fusion.13 = (bf16[256,8,128]{2,1,0:T(8,128)(2,1)}, bf16[256,8,128]{2,1,0:T(8,128)(2,1)}) fusion(bf16[256,4,128]{2,1,0:T(4,128)(2,1)S(1)} %get-tuple-element.1134, bf16[8,4]{0,1:T(4,128)(2,1)S(1)} %fusion.119, bf16[256,4,128]{2,1,0:T(4,128)(2,1)S(1)} %get-tuple-element.1135), kind=kLoop, calls=%fused_computation.37.clone.1 | loop fusion | flops 3670016 | bytes 1572928 | tf_op jit(solution)/shard_map/while/body/eval_jaxpr/reduce_sum | solution.py:39
  84.5 3.4 %fusion.120 = f32[256,8,128]{0,2,1:T(8,128)} fusion(bf16[256,8,128]{2,0,1:T(8,128)(2,1)S(1)} %get-tuple-element.1236, f32[256,8,128]{0,2,1:T(8,128)} %get-tuple-element.1216, f32[8,256]{1,0:T(8,128)S(1)} %get-tuple-element.1237, pred[256,256]{0,1:T(8,128)(4,1)S(1)} %fusion.118, bf16[256,8,128]{2,1,0:T(8,128)(2,1)} %get-tuple-element.1136, ...), kind=kOutput, calls=%fused_computation.41.clone.1 | convolution fusion | flops 271056896 | bytes 3743745 | tf_op jit(solution)/shard_map/while/body/eval_jaxpr/hqk,khd->qhd/dot_general | solution.py:98
  90.0 3.0 %multiply_reduce_fusion.13 = (bf16[256,8,128]{2,1,0:T(8,128)(2,1)}, bf16[256,8,128]{2,1,0:T(8,128)(2,1)}) fusion(bf16[256,4,128]{2,1,0:T(4,128)(2,1)S(1)} %get-tuple-element.1134, bf16[8,4]{0,1:T(4,128)(2,1)S(1)} %fusion.119, bf16[256,4,128]{2,1,0:T(4,128)(2,1)S(1)} %get-tuple-element.1135), kind=kLoop, calls=%fused_computation.37.clone.1 | loop fusion | flops 3670016 | bytes 1572928 | tf_op jit(solution)/shard_map/while/body/eval_jaxpr/reduce_sum | solution.py:39
  93.0 3.4 %fusion.120 = f32[256,8,128]{0,2,1:T(8,128)} fusion(bf16[256,8,128]{2,0,1:T(8,128)(2,1)S(1)} %get-tuple-element.1236, f32[256,8,128]{0,2,1:T(8,128)} %get-tuple-element.1216, f32[8,256]{1,0:T(8,128)S(1)} %get-tuple-element.1237, pred[256,256]{0,1:T(8,128)(4,1)S(1)} %fusion.118, bf16[256,8,128]{2,1,0:T(8,128)(2,1)} %get-tuple-element.1136, ...), kind=kOutput, calls=%fused_computation.41.clone.1 | convolution fusion | flops 271056896 | bytes 3743745 | tf_op jit(solution)/shard_map/while/body/eval_jaxpr/hqk,khd->qhd/dot_general | solution.py:98
  98.5 3.0 %multiply_reduce_fusion.13 = (bf16[256,8,128]{2,1,0:T(8,128)(2,1)}, bf16[256,8,128]{2,1,0:T(8,128)(2,1)}) fusion(bf16[256,4,128]{2,1,0:T(4,128)(2,1)S(1)} %get-tuple-element.1134, bf16[8,4]{0,1:T(4,128)(2,1)S(1)} %fusion.119, bf16[256,4,128]{2,1,0:T(4,128)(2,1)S(1)} %get-tuple-element.1135), kind=kLoop, calls=%fused_computation.37.clone.1 | loop fusion | flops 3670016 | bytes 1572928 | tf_op jit(solution)/shard_map/while/body/eval_jaxpr/reduce_sum | solution.py:39
  101.5 3.4 %fusion.120 = f32[256,8,128]{0,2,1:T(8,128)} fusion(bf16[256,8,128]{2,0,1:T(8,128)(2,1)S(1)} %get-tuple-element.1236, f32[256,8,128]{0,2,1:T(8,128)} %get-tuple-element.1216, f32[8,256]{1,0:T(8,128)S(1)} %get-tuple-element.1237, pred[256,256]{0,1:T(8,128)(4,1)S(1)} %fusion.118, bf16[256,8,128]{2,1,0:T(8,128)(2,1)} %get-tuple-element.1136, ...), kind=kOutput, calls=%fused_computation.41.clone.1 | convolution fusion | flops 271056896 | bytes 3743745 | tf_op jit(solution)/shard_map/while/body/eval_jaxpr/hqk,khd->qhd/dot_general | solution.py:98
  104.9 2.4 copy.55
  107.3 1.5 multiply_reduce_fusion.7
  108.9 53.1 %while.52 = (s32[]{:T(128)}, f32[256,8,128]{0,2,1:T(8,128)}, f32[4,2,256,4,128]{4,3,2,1,0:T(4,128)}, bf16[4,2,256,4,128]{4,3,2,1,0:T(4,128)(2,1)S(1)}, s32[4]{0:...) while((s32[]{:T(128)}, f32[256,8,128]{0,2,1:T(8,128)}, ...), condition=%wide.region_18.19_spmd.clone.clone.clone.clone, body=%wide.region_12.18_spmd.clone.clone.clone.clone.sunk | while | flops 684065344 | bytes 55727124 | solution.py:133
  111.3 1.7 multiply_reduce_fusion.14
  113.3 0.7 fusion.134
  117.2 3.1 %multiply_reduce_fusion.15 = (f32[256,4,128]{2,1,0:T(4,128)S(1)}, f32[256,4,128]{2,1,0:T(4,128)S(1)}) fusion(f32[8,4]{0,1:T(4,128)S(1)} %get-tuple-element.1155, f32[256,8,128]{2,1,0:T(8,128)S(1)} %copy.106, f32[256,8,128]{2,1,0:T(8,128)S(1)} %copy.107), kind=kLoop, calls=%fused_computation.69.clone.1 | loop fusion | flops 3932160 | bytes 3145856 | tf_op jit(solution)/shard_map/while/body/eval_jaxpr/reduce_sum | solution.py:42
  120.3 1.2 fusion.138
  121.6 0.7 copy-done.4
  124.5 1.7 multiply_reduce_fusion.14
  126.6 0.7 fusion.134
  130.5 3.1 %multiply_reduce_fusion.15 = (f32[256,4,128]{2,1,0:T(4,128)S(1)}, f32[256,4,128]{2,1,0:T(4,128)S(1)}) fusion(f32[8,4]{0,1:T(4,128)S(1)} %get-tuple-element.1155, f32[256,8,128]{2,1,0:T(8,128)S(1)} %copy.106, f32[256,8,128]{2,1,0:T(8,128)S(1)} %copy.107), kind=kLoop, calls=%fused_computation.69.clone.1 | loop fusion | flops 3932160 | bytes 3145856 | tf_op jit(solution)/shard_map/while/body/eval_jaxpr/reduce_sum | solution.py:42
  133.6 1.3 fusion.138
  134.9 0.7 copy-done.4
  137.7 1.7 multiply_reduce_fusion.14
  139.8 0.7 fusion.134
  143.7 3.1 %multiply_reduce_fusion.15 = (f32[256,4,128]{2,1,0:T(4,128)S(1)}, f32[256,4,128]{2,1,0:T(4,128)S(1)}) fusion(f32[8,4]{0,1:T(4,128)S(1)} %get-tuple-element.1155, f32[256,8,128]{2,1,0:T(8,128)S(1)} %copy.106, f32[256,8,128]{2,1,0:T(8,128)S(1)} %copy.107), kind=kLoop, calls=%fused_computation.69.clone.1 | loop fusion | flops 3932160 | bytes 3145856 | tf_op jit(solution)/shard_map/while/body/eval_jaxpr/reduce_sum | solution.py:42
  146.8 1.2 fusion.138
  148.0 0.7 copy-done.4
  151.0 1.7 multiply_reduce_fusion.14
  153.0 0.7 fusion.134
  156.9 3.1 %multiply_reduce_fusion.15 = (f32[256,4,128]{2,1,0:T(4,128)S(1)}, f32[256,4,128]{2,1,0:T(4,128)S(1)}) fusion(f32[8,4]{0,1:T(4,128)S(1)} %get-tuple-element.1155, f32[256,8,128]{2,1,0:T(8,128)S(1)} %copy.106, f32[256,8,128]{2,1,0:T(8,128)S(1)} %copy.107), kind=kLoop, calls=%fused_computation.69.clone.1 | loop fusion | flops 3932160 | bytes 3145856 | tf_op jit(solution)/shard_map/while/body/eval_jaxpr/reduce_sum | solution.py:42
  160.0 1.2 fusion.138
  161.3 0.7 copy-done.4
  162.0 3.5 %fusion.65 = (f32[1,2,256,4,128]{4,3,2,1,0:T(4,128)S(1)}, f32[1,2,256,4,128]{4,3,2,1,0:T(4,128)S(1)}, f32[1,2,256,4,128]{4,3,2,1,0:T(4,128)}, f32[1,2,256,4,128]{4,3,2,1,0:T(4,128)S(1)}) fusion(f32[4,2,256,4,128]{4,3,2,1,0:T(4,128)} %get-tuple-element.502), kind=kLoop, calls=%fused_computation.116 | loop fusion | bytes 8388608 | tf_op jit(solution)/shard_map/slice | solution.py:138
  165.4 1.4 squeeze.36
  166.9 1.9 collective-permute-start.3
  168.8 1.6 squeeze.37
  170.4 19.9 %collective-permute-done.3 = f32[2,256,512]{2,1,0:T(8,128)} collective-permute-done((f32[2,256,512]{2,1,0:T(8,128)}, f32[2,256,512]{2,1,0:T(8,128)}, u32[]{:S(2)}, u32[]{:S(2)}) %collective-permute-start.3) | collective-permute-done | bytes 1048608 | tf_op jit(solution)/shard_map/ppermute | solution.py:20
  190.3 2.4 add.160
  192.7 2.2 collective-permute-start.4
  195.4 19.9 %collective-permute-done.4 = f32[2,256,512]{2,1,0:T(8,128)} collective-permute-done((f32[2,256,512]{2,1,0:T(8,128)}, f32[2,256,512]{2,1,0:T(8,128)}, u32[]{:S(2)}, u32[]{:S(2)}) %collective-permute-start.4) | collective-permute-done | bytes 1048608 | tf_op jit(solution)/shard_map/ppermute | solution.py:20
  215.3 2.4 add.161
  217.7 2.5 collective-permute-start.5
  220.6 18.7 %collective-permute-done.5 = f32[2,256,512]{2,1,0:T(8,128)} collective-permute-done((f32[2,256,512]{2,1,0:T(8,128)}, f32[2,256,512]{2,1,0:T(8,128)}, u32[]{:S(2)}, u32[]{:S(2)}) %collective-permute-start.5) | collective-permute-done | bytes 1048608 | tf_op jit(solution)/shard_map/ppermute | solution.py:20
  239.3 2.2 add_convert_fusion
  241.5 1.2 copy.59
  242.7 24.0 %all-reduce.2.cloned.1.call-done = bf16[2,256,512]{2,1,0:T(8,128)(2,1)} async-done(((bf16[2,256,512]{2,1,0:T(8,128)(2,1)}), bf16[2,256,512]{2,1,0:T(8,128)(2,1)}) %all-reduce.2.cloned.1.call-update) | async-done | bytes 524304 | tf_op jit(solution)/shard_map/psum | solution.py:139
  266.7 1.1 fusion.66
  267.8 0.8 reshape_squeeze.7
  268.5 0.8 reshape_squeeze.6
  (247 shorter events, 35.2 us)
Async XLA Ops:
  7.2 35.2 %copy-start.5 = (bf16[256,8,128]{2,1,0:T(8,128)(2,1)S(1)}, bf16[256,8,128]{2,1,0:T(8,128)(2,1)}, u32[]{:S(2)}) copy-start(bf16[256,8,128]{2,1,0:T(8,128)(2,1)} %param.14) | copy-start | bytes 1572868
  7.2 259.5 %all-reduce.2.cloned.1.call-start = ((), (), s32[]{:S(2)}) async-start(), calls=%async_computation | async-start | bytes 1048576 | tf_op jit(solution)/shard_map/psum | solution.py:139
  9.5 14.7 %collective-permute-start = (bf16[2,256,4,128]{3,2,1,0:T(4,128)(2,1)S(1)}, bf16[2,256,4,128]{3,2,1,0:T(4,128)(2,1)S(1)}, u32[]{:S(2)}, u32[]{:S(2)}) collective-permute-start(bf16[2,256,4,128]{3,2,1,0:T(4,128)(2,1)S(1)} %get-tuple-element.945), channel_id=1, source_target_pairs={{0,4},{4,8},{8,12},{1,5},{5,9},{9,13},{2,6},{6,10},{10,14},{3,7},{... | collective-permute-start | bytes 1572872 | tf_op jit(solution)/shard_map/ppermute | solution.py:20
  24.2 26.6 %copy-start.6 = (bf16[2,256,4,128]{3,2,1,0:T(4,128)(2,1)}, bf16[2,256,4,128]{3,2,1,0:T(4,128)(2,1)S(1)}, u32[]{:S(2)}) copy-start(bf16[2,256,4,128]{3,2,1,0:T(4,128)(2,1)S(1)} %collective-permute-done) | copy-start | bytes 1572868
  24.2 13.8 %collective-permute-start.1 = (bf16[2,256,4,128]{3,2,1,0:T(4,128)(2,1)S(1)}, bf16[2,256,4,128]{3,2,1,0:T(4,128)(2,1)S(1)}, u32[]{:S(2)}, u32[]{:S(2)}) collective-permute-start(bf16[2,256,4,128]{3,2,1,0:T(4,128)(2,1)S(1)} %collective-permute-done), channel_id=1, source_target_pairs={{0,4},{4,8},{8,12},{1,5},{5,9},{9,13},{2,6},{6,10},{10,14},{3,7},{... | collective-permute-start | bytes 1572872 | tf_op jit(solution)/shard_map/ppermute | solution.py:20
  37.9 12.8 %copy-start.7 = (bf16[2,256,4,128]{3,2,1,0:T(4,128)(2,1)}, bf16[2,256,4,128]{3,2,1,0:T(4,128)(2,1)S(1)}, u32[]{:S(2)}) copy-start(bf16[2,256,4,128]{3,2,1,0:T(4,128)(2,1)S(1)} %collective-permute-done.1) | copy-start | bytes 1572868
  37.9 12.8 %collective-permute-start.2 = (bf16[2,256,4,128]{3,2,1,0:T(4,128)(2,1)S(1)}, bf16[2,256,4,128]{3,2,1,0:T(4,128)(2,1)S(1)}, u32[]{:S(2)}, u32[]{:S(2)}) collective-permute-start(bf16[2,256,4,128]{3,2,1,0:T(4,128)(2,1)S(1)} %collective-permute-done.1), channel_id=1, source_target_pairs={{0,4},{4,8},{8,12},{1,5},{5,9},{9,13},{2,6},{6,10},{10,14},{3,7},{... | collective-permute-start | bytes 1572872 | tf_op jit(solution)/shard_map/ppermute | solution.py:20
  50.8 0.8 copy-start.8
  51.6 3.2 %copy-start.9 = (s32[2,17]{1,0:T(2,128)S(1)}, s32[2,17]{1,0:T(2,128)}, u32[]{:S(2)}) copy-start(s32[2,17]{1,0:T(2,128)} %param.15) | copy-start | bytes 412
  109.1 2.2 copy-start.3
  114.5 1.2 copy-start
  116.2 1.1 copy-start.1
  120.3 2.0 copy-start.4
  122.3 2.2 copy-start.3
  127.7 1.2 copy-start
  129.4 1.1 copy-start.1
  133.6 2.0 copy-start.4
  135.5 2.2 copy-start.3
  140.9 1.2 copy-start
  142.6 1.1 copy-start.1
  146.8 2.0 copy-start.4
  148.8 2.2 copy-start.3
  154.2 1.2 copy-start
  155.8 1.1 copy-start.1
  160.0 2.0 copy-start.4
  166.9 23.5 %collective-permute-start.3 = (f32[2,256,512]{2,1,0:T(8,128)}, f32[2,256,512]{2,1,0:T(8,128)}, u32[]{:S(2)}, u32[]{:S(2)}) collective-permute-start(f32[2,256,512]{2,1,0:T(8,128)} %squeeze.36), channel_id=1, source_target_pairs={{4,0},{8,4},{12,8},{5,1},{9,5},{13,9},{6,2},{10,6},{14,10},{7,3},{... | collective-permute-start | bytes 3145736 | tf_op jit(solution)/shard_map/ppermute | solution.py:20
  192.7 22.5 %collective-permute-start.4 = (f32[2,256,512]{2,1,0:T(8,128)}, f32[2,256,512]{2,1,0:T(8,128)}, u32[]{:S(2)}, u32[]{:S(2)}) collective-permute-start(f32[2,256,512]{2,1,0:T(8,128)} %add.160), channel_id=1, source_target_pairs={{4,0},{8,4},{12,8},{5,1},{9,5},{13,9},{6,2},{10,6},{14,10},{7,3},{... | collective-permute-start | bytes 3145736 | tf_op jit(solution)/shard_map/ppermute | solution.py:20
  217.7 21.6 %collective-permute-start.5 = (f32[2,256,512]{2,1,0:T(8,128)}, f32[2,256,512]{2,1,0:T(8,128)}, u32[]{:S(2)}, u32[]{:S(2)}) collective-permute-start(f32[2,256,512]{2,1,0:T(8,128)} %add.161), channel_id=1, source_target_pairs={{4,0},{8,4},{12,8},{5,1},{9,5},{13,9},{6,2},{10,6},{14,10},{7,3},{... | collective-permute-start | bytes 3145736 | tf_op jit(solution)/shard_map/ppermute | solution.py:20
  220.6 20.9 %copy-start.2 = (f32[256,8,128]{0,2,1:T(8,128)S(1)}, f32[256,8,128]{0,2,1:T(8,128)}, u32[]{:S(2)}) copy-start(f32[256,8,128]{0,2,1:T(8,128)} %get-tuple-element.501) | copy-start | bytes 3145732
Sparse Core Ops, SparseCore 0:
  241.6 25.0 all-reduce.1
where the time goes:
time: 278 us; the launch traced here: 276 us
  waiting for transfers between devices  113 us (41%)
  other arithmetic  61.5 us (22%)
  local copies, waits for them, and re-layouts  37 us (13%)
  matrix products  25 us (9%)
  starting transfers between devices  16.2 us (6%)
  between operations  14.3 us (5%)
  loops' own time  9.39 us (3%)
    ppermute x6, waiting for transfers between devices, from_behind(): lax.ppermute(value, axis, [(source, source + steps) for source in range(f...  88.9 us
    psum x1, waiting for transfers between devices, body(): summed = lax.psum(moving.astype(jnp.bfloat16), 'sub')  24 us
    reduce_sum x12, other arithmetic, widen(): return jnp.sum(states[:, None, :, :] * pick_low[None, :, :, None], axis=2)  23.4 us
    ppermute x6, starting transfers between devices, from_behind(): lax.ppermute(value, axis, [(source, source + steps) for source in range(f...  16.1 us
    dot_general x4, matrix products, add_values(): jnp.einsum('hqk,khd->qhd', weights, widen(pair_now[1]), preferred_element...  13.3 us
    reduce_sum x4, other arithmetic, narrow(): return jnp.sum(terms[:, :, None, :] * pick_wide[None, :, :, None], axis=1)  12.4 us
    dynamic_slice x12, local copies, waits for them, and re-layouts, body(): lax.scan(gather_stats, start_stats, (slot_numbers, stacked))  7.35 us
  transfers between devices with their start and end apart: 7, of which 7 were waited for; matrix products, arithmetic and copies ran while one was open for 2% of the time, Pallas kernels for 0%

commit v1 on v0

v1 whole, which is shorter than its diff:
```python
import functools
import math

import jax
import jax.numpy as jnp
from jax import lax
from jax.experimental import pallas as pl
from jax.experimental.pallas import tpu as pltpu
from jax.sharding import PartitionSpec as P

HEADS = 32
KV_HEADS = 8
BLOCK = 128
WINDOW = 2048
NEGATIVE = -1e30
LOG2E = 1.4426950408889634

VMEM = pl.BlockSpec(memory_space=pltpu.VMEM)
SMEM = pl.BlockSpec(memory_space=pltpu.SMEM)


def shifted(value, axis, steps):
    count = lax.axis_size(axis)
    first, last = (max(0, -steps), min(count, count - steps))
    return lax.ppermute(value, axis, [(source, source + steps) for source in range(first, last)])


def dot(left, right):
    return jnp.dot(left, right, preferred_element_type=jnp.float32)


def pack_kernel(rows, kv_heads, used, meta, key_in, value_in, *refs):
    outs, wide = (refs[:used], refs[used])
    first = meta[1]
    for place, source in enumerate((key_in, value_in)):
        wide[...] = source[...].astype(jnp.float32)
        for head in range(used):
            picked = wide[pl.ds(first + head, rows, stride=kv_heads), :]
            outs[head][place] = picked.astype(jnp.bfloat16)


def turn_kernel(rows, q_heads, used, query_in, grad_in, *refs):
    outs, wide = (refs[: 4 * used], refs[4 * used])
    per = q_heads // used
    for place, source in enumerate((query_in, grad_in)):
        wide[...] = source[...].astype(jnp.float32)
        for head in range(q_heads):
            picked = wide[pl.ds(head, rows, stride=q_heads), :]
            slot, local = divmod(head, per)
            straight, flipped = outs[4 * slot + 2 * place : 4 * slot + 2 * place + 2]
            straight[pl.ds(local * rows, rows), :] = picked.astype(jnp.bfloat16)
            flipped[:, pl.ds(local * rows, rows)] = picked.T.astype(jnp.bfloat16)


def attend_kernel(rows, per, lags, meta, mask, q_ref, qt_ref, g_ref, gt_ref, *refs):
    pairs = refs[:lags]
    out_ref, qgrad_ref, own_ref = refs[lags : lags + 3]
    terms = refs[lags + 3 : 2 * lags + 2]
    scores, weights, slopes, row_max, row_sum, out_t, qgrad_t = refs[2 * lags + 2 :]
    shard = meta[0]
    blocks = rows // BLOCK
    head_size = q_ref.shape[1]
    scale = 1.0 / math.sqrt(head_size)
    to_exp2 = scale * LOG2E

    def each_lag(step):
        for lag in range(lags):
            if lag == 0:
                step(lag)
            else:
                pl.when(shard >= lag)(functools.partial(step, lag))

    def columns(head):
        return pl.ds(head * rows, rows)

    def fold(op, tile):
        return op(tile.reshape(rows // 8, 8, rows), axis=0)

    row_max[...] = jnp.full(row_max.shape, NEGATIVE, jnp.float32)
    row_sum[...] = jnp.zeros(row_sum.shape, jnp.float32)
    out_t[...] = jnp.zeros(out_t.shape, jnp.float32)
    qgrad_t[...] = jnp.zeros(qgrad_t.shape, jnp.float32)

    def score_step(lag):
        key_pos = lax.broadcasted_iota(jnp.int32, (rows, rows), 0)
        query_pos = lax.broadcasted_iota(jnp.int32, (rows, rows), 1)
        query_block = lax.broadcasted_iota(jnp.int32, (1, rows), 1) // BLOCK
        biases = []
        for key_block in range(blocks):
            bias = jnp.full((1, rows), NEGATIVE, jnp.float32)
            for block in range(blocks):
                distance = lag * blocks + block - key_block
                if 0 <= distance < mask.shape[1]:
                    shown = jnp.where(mask[block, distance] > 0, 0.0, NEGATIVE)
                    bias = jnp.where(query_block == block, shown, bias)
            biases.append(jnp.broadcast_to(bias, (BLOCK, rows)))
        bias = jnp.concatenate(biases, 0)
        gap = query_pos - key_pos + lag * rows
        if lag == 0:
            bias = jnp.where(gap >= 0, bias, NEGATIVE)
        if (lag + 1) * rows > WINDOW:
            bias = jnp.where(gap < WINDOW, bias, NEGATIVE)
        for head in range(per):
            tile = dot(pairs[lag][0], qt_ref[:, columns(head)]) + bias
            scores[lag, :, columns(head)] = tile
            row_max[:, columns(head)] = jnp.maximum(row_max[:, columns(head)], fold(jnp.max, tile))

    each_lag(score_step)
    top = jnp.max(row_max[...], axis=0, keepdims=True) * to_exp2

    def exp_step(lag):
        for head in range(per):
            tile = jnp.exp2(
                scores[lag, :, columns(head)] * to_exp2 - top[:, head * rows : (head + 1) * rows]
            )
            scores[lag, :, columns(head)] = tile
            row_sum[:, columns(head)] += fold(jnp.sum, tile)

    each_lag(exp_step)
    share = 1.0 / jnp.sum(row_sum[...], axis=0, keepdims=True)

    def value_step(lag):
        value_t = pairs[lag][1].T
        for head in range(per):
            tile = scores[lag, :, columns(head)] * share[:, head * rows : (head + 1) * rows]
            scores[lag, :, columns(head)] = tile
            low = tile.astype(jnp.bfloat16)
            weights[:, columns(head)] = low
            out_t[:, columns(head)] += dot(value_t, low)
        part = dot(weights[...], g_ref[...])
        if lag == 0:
            own_ref[1] = part
        else:
            terms[lag - 1][1] = part.astype(jnp.bfloat16)

    each_lag(value_step)
    attended_t = out_t[...].astype(jnp.bfloat16).astype(jnp.float32)
    drift = jnp.sum(attended_t * gt_ref[...].astype(jnp.float32), axis=0, keepdims=True)
    out_ref[...] = attended_t.T.astype(jnp.bfloat16)

    def slope_step(lag):
        key_t = pairs[lag][0].T
        for head in range(per):
            pushed = dot(pairs[lag][1], gt_ref[:, columns(head)])
            tile = scores[lag, :, columns(head)] * (
                pushed - drift[:, head * rows : (head + 1) * rows]
            )
            low = tile.astype(jnp.bfloat16)
            slopes[:, columns(head)] = low
            qgrad_t[:, columns(head)] += dot(key_t, low)
        part = dot(slopes[...], q_ref[...]) * scale
        if lag == 0:
            own_ref[0] = part
        else:
            terms[lag - 1][0] = part.astype(jnp.bfloat16)

    each_lag(slope_step)
    qgrad_ref[...] = (qgrad_t[...] * scale).T.astype(jnp.bfloat16)


def unturn_kernel(rows, q_heads, used, *refs):
    sources, outs, wide = (refs[: 2 * used], refs[2 * used : 2 * used + 2], refs[-1])
    per = q_heads // used
    for place, target in enumerate(outs):
        for head in range(q_heads):
            slot, local = divmod(head, per)
            tile = sources[2 * slot + place][pl.ds(local * rows, rows), :]
            wide[pl.ds(head, rows, stride=q_heads), :] = tile.astype(jnp.float32)
        target[...] = wide[...].astype(jnp.bfloat16)


def join_kernel(rows, kv_heads, used, meta, *refs):
    own, other = (refs[:used], refs[used : 2 * used])
    outs, wide = (refs[2 * used : 2 * used + 2], refs[-1])
    first = meta[1]
    for place, target in enumerate(outs):
        for head in range(used):
            mine = own[head][place].astype(jnp.float32)
            theirs = other[head][place].astype(jnp.float32)
            if used == kv_heads:
                wide[pl.ds(head, rows, stride=kv_heads), :] = mine + theirs
            else:
                away = kv_heads - used - first
                wide[pl.ds(first + head, rows, stride=kv_heads), :] = mine
                wide[pl.ds(away + head, rows, stride=kv_heads), :] = theirs
        target[...] = wide[...].astype(jnp.bfloat16)


def body(query, key_states, value_states, grad_out, block_mask):
    rows, q_heads, head_size = query.shape
    kv_heads = key_states.shape[1]
    lags = min(WINDOW // rows, lax.axis_size("seq") - 1) + 1
    used = max(1, q_heads * KV_HEADS // HEADS)
    per = q_heads // used
    width = per * rows
    low, wide = (jnp.bfloat16, jnp.float32)
    core_first = lax.axis_index("sub") * q_heads * KV_HEADS // HEADS
    meta = jnp.stack([lax.axis_index("seq"), core_first]).astype(jnp.int32)
    params = pltpu.CompilerParams(vmem_limit_bytes=28 * 2**20)

    def call(kernel, ins, outs, scratch, flops=0, moved=2**20):
        return pl.pallas_call(
            kernel,
            in_specs=ins,
            out_specs=[VMEM] * len(outs),
            out_shape=[jax.ShapeDtypeStruct(*o) for o in outs],
            scratch_shapes=[pltpu.VMEM(*s) for s in scratch],
            compiler_params=params,
            cost_estimate=pl.CostEstimate(flops=flops, bytes_accessed=moved, transcendentals=0),
        )

    packed = call(
        functools.partial(pack_kernel, rows, kv_heads, used),
        [SMEM, VMEM, VMEM],
        [((2, rows, head_size), low)] * used,
        [((rows * kv_heads, head_size), wide)],
    )(meta, key_states.reshape(-1, head_size), value_states.reshape(-1, head_size))
    pairs = [[pair] + [shifted(pair, "seq", lag) for lag in range(1, lags)] for pair in packed]

    turned = call(
        functools.partial(turn_kernel, rows, q_heads, used),
        [VMEM, VMEM],
        [((width, head_size), low), ((head_size, width), low)] * (2 * used),
        [((rows * q_heads, head_size), wide)],
    )(query.reshape(-1, head_size), grad_out.reshape(-1, head_size))

    results, sums = ([], [])
    for head in range(used):
        attended, qgrad, own, *terms = call(
            functools.partial(attend_kernel, rows, per, lags),
            [SMEM, SMEM] + [VMEM] * (4 + lags),
            [((width, head_size), low)] * 2
            + [((2, rows, head_size), wide)]
            + [((2, rows, head_size), low)] * (lags - 1),
            [
                ((lags, rows, width), wide),
                ((rows, width), low),
                ((rows, width), low),
                ((8, width), wide),
                ((8, width), wide),
                ((head_size, width), wide),
                ((head_size, width), wide),
            ],
            flops=12 * lags * rows * width * head_size,
        )(meta, block_mask, *turned[4 * head : 4 * head + 4], *pairs[head])
        results += [attended, qgrad]
        for lag in range(lags - 1, 0, -1):
            own = own + shifted(terms[lag - 1], "seq", -lag).astype(wide)
        sums.append(own.astype(low))

    attended, qgrad = call(
        functools.partial(unturn_kernel, rows, q_heads, used),
        [VMEM] * (2 * used),
        [((rows * q_heads, head_size), low)] * 2,
        [((rows * q_heads, head_size), wide)],
    )(*results)
    others = [lax.ppermute(value, "sub", [(0, 1), (1, 0)]) for value in sums]
    key_grad, value_grad = call(
        functools.partial(join_kernel, rows, kv_heads, used),
        [SMEM] + [VMEM] * (2 * used),
        [((rows * kv_heads, head_size), low)] * 2,
        [((rows * kv_heads, head_size), wide)],
    )(meta, *sums, *others)
    return (
        attended.reshape(rows, q_heads, head_size),
        qgrad.reshape(rows, q_heads, head_size),
        key_grad.reshape(rows, kv_heads, head_size),
        value_grad.reshape(rows, kv_heads, head_size),
    )


def solution(mesh):
    q_spec = P(("groups", "seq"), ("tensor", "sub"), None)
    kv_spec = P(("groups", "seq"), "tensor", None)
    return jax.shard_map(
        body,
        mesh=mesh,
        in_specs=(q_spec, kv_spec, kv_spec, q_spec, P(("groups", "seq"), None)),
        out_specs=(q_spec, q_spec, kv_spec, kv_spec),
        check_vma=False,
    )
```

time: 278 us -> 56.6 us (0.20)
  waiting for transfers between devices: 113 us -> 12.3 us
  other arithmetic: 61.5 us -> 0.22 us
  local copies, waits for them, and re-layouts: 37 us -> 3.67 us
  matrix products: 25 us -> 0 us
  Pallas kernels: 0 us -> 13.9 us
  between operations: 14.3 us -> 0.84 us
  loops' own time: 9.39 us -> 0 us
  starting transfers between devices: 16.2 us -> 24.7 us
    ppermute x6 -> x14, waiting for transfers between devices: 88.9 us -> 12.3 us  [the longest x12 12.3 us: shifted(): lax.ppermute(value, axis, [(source, source + steps) for source in range(f...]
    reduce_sum x33 -> x0, other arithmetic: 41.6 us -> none  [the longest x12 23.4 us: widen(): return jnp.sum(states[:, None, :, :] * pick_low[None, :, :, None], axis=2)]
    dot_general x28 -> x0, matrix products: 25 us -> none  [the longest x4 13.3 us: add_values(): jnp.einsum('hqk,khd->qhd', weights, widen(pair_now[1]), preferred_element...]
    psum x1 -> x0, waiting for transfers between devices: 24 us -> none  [body(): summed = lax.psum(moving.astype(jnp.bfloat16), 'sub')]
    pallas_call x0 -> x6, Pallas kernels: none -> 13.9 us  [the longest x2 9.78 us: body(): call(functools.partial(attend_kernel, rows, per, lags), [SMEM, SMEM] + [V...]
    another operation x3 -> x0, loops' own time: 9.39 us -> none  [the longest x1 3.54 us: body(): lax.scan(backward_tile, zero_rows, (slot_numbers, stacked))]
    ppermute x6 -> x14, starting transfers between devices: 16.1 us -> 24.7 us  [the longest x12 18.1 us: shifted(): lax.ppermute(value, axis, [(source, source + steps) for source in range(f...]
    while x62 -> x0, local copies, waits for them, and re-layouts: 8.16 us -> none
  transfers between devices with their start and end apart: 7 -> 14, of which waited for: 7 -> 5; matrix products, arithmetic and copies ran while one was open for 2% -> 0% of each run, Pallas kernels for 0% -> 21%
where the time goes in v1:
time: 56.6 us; the launch traced here: 55.7 us
  starting transfers between devices  24.7 us (44%)
  Pallas kernels  13.9 us (25%)
  waiting for transfers between devices  12.3 us (22%)
  local copies, waits for them, and re-layouts  3.67 us (6%)
  between operations  0.84 us (1%)
    ppermute x12, starting transfers between devices, shifted(): lax.ppermute(value, axis, [(source, source + steps) for source in range(f...  18.1 us
    ppermute x12, waiting for transfers between devices, shifted(): lax.ppermute(value, axis, [(source, source + steps) for source in range(f...  12.3 us
    pallas_call x2, Pallas kernels, body(): call(functools.partial(attend_kernel, rows, per, lags), [SMEM, SMEM] + [V...  9.78 us
    ppermute x2, starting transfers between devices, body(): others = [lax.ppermute(value, 'sub', [(0, 1), (1, 0)]) for value in sums]  6.65 us
    unnamed x10, local copies, waits for them, and re-layouts  3.67 us
    pallas_call x1, Pallas kernels, body(): call(functools.partial(join_kernel, rows, kv_heads, used), [SMEM] + [VMEM...  1.5 us
    pallas_call x1, Pallas kernels, body(): call(functools.partial(unturn_kernel, rows, q_heads, used), [VMEM] * (2 *...  1.47 us
  transfers between devices with their start and end apart: 14, of which 5 were waited for; matrix products, arithmetic and copies ran while one was open for 0% of the time, Pallas kernels for 21%

profile of v1, /device:TPU:13, one launch (start us, length us, event | category | flops | bytes accessed | tf_op | source)
XLA Modules:
  0.0 55.7 jit_solution(8380045596518540429)
XLA Ops:
  0.6 0.0 copy-start
  0.7 0.1 pad_add_fusion.meta
  0.7 0.0 copy-start.2
  0.7 1.0 %copy-done.2 = bf16[256,4,128]{2,1,0:T(4,128)(2,1)S(1)} copy-done((bf16[256,4,128]{2,1,0:T(4,128)(2,1)S(1)}, bf16[256,4,128]{2,1,0:T(4,128)(2,1)}, u32[]{:S(2)}) %copy-start.2) | copy-done | bytes 262168
  1.7 0.0 copy-start.3
  1.7 0.9 %copy-done.3 = bf16[256,4,128]{2,1,0:T(4,128)(2,1)S(1)} copy-done((bf16[256,4,128]{2,1,0:T(4,128)(2,1)S(1)}, bf16[256,4,128]{2,1,0:T(4,128)(2,1)}, u32[]{:S(2)}) %copy-start.3) | copy-done | bytes 262168
  2.7 0.7 %shard_map.85 = (bf16[2,256,128]{2,1,0:T(8,128)(2,1)S(1)}, bf16[2,256,128]{2,1,0:T(8,128)(2,1)S(1)}) custom-call(s32[2]{0:T(128)S(1)} %pad_add_fusion.meta, bf16[1024,128]{1,0:T(8,128)(2,1)S(1)} %bitcast.12, bf16[1024,128]{1,0:T(8,128)(2,1)S(1)} %bitcast.13), custom_call_target="tpu_custom_call" | custom-call | bytes 1048576 | tf_op jit(solution)/shard_map/pallas_call | solution.py:212
  3.3 3.2 %collective-permute-start.3 = (bf16[2,256,128]{2,1,0:T(8,128)(2,1)S(1)}, bf16[2,256,128]{2,1,0:T(8,128)(2,1)S(1)}, u32[]{:S(2)}, u32[]{:S(2)}) collective-permute-start(bf16[2,256,128]{2,1,0:T(8,128)(2,1)S(1)} %get-tuple-element.41.refs_0_), channel_id=1, source_target_pairs={{0,4},{4,8},{8,12},{1,5},{5,9},{9,13},{2,6},{6,10},{10,14},{3,7},{... | collective-permute-start | bytes 393224 | tf_op jit(solution)/shard_map/ppermute | solution.py:25
  6.6 2.3 %collective-permute-start.4 = (bf16[2,256,128]{2,1,0:T(8,128)(2,1)S(1)}, bf16[2,256,128]{2,1,0:T(8,128)(2,1)S(1)}, u32[]{:S(2)}, u32[]{:S(2)}) collective-permute-start(bf16[2,256,128]{2,1,0:T(8,128)(2,1)S(1)} %get-tuple-element.41.refs_0_), channel_id=1, source_target_pairs={{0,8},{4,12},{1,9},{5,13},{2,10},{6,14},{3,11},{7,15},{16,24},{20,... | collective-permute-start | bytes 393224 | tf_op jit(solution)/shard_map/ppermute | solution.py:25
  8.9 0.7 %collective-permute-start.5 = (bf16[2,256,128]{2,1,0:T(8,128)(2,1)S(1)}, bf16[2,256,128]{2,1,0:T(8,128)(2,1)S(1)}, u32[]{:S(2)}, u32[]{:S(2)}) collective-permute-start(bf16[2,256,128]{2,1,0:T(8,128)(2,1)S(1)} %get-tuple-element.41.refs_0_), channel_id=1, source_target_pairs={{0,12},{1,13},{2,14},{3,15},{16,28},{17,29},{18,30},{19,31}} | collective-permute-start | bytes 393224 | tf_op jit(solution)/shard_map/ppermute | solution.py:25
  9.6 2.2 %collective-permute-start = (bf16[2,256,128]{2,1,0:T(8,128)(2,1)S(1)}, bf16[2,256,128]{2,1,0:T(8,128)(2,1)S(1)}, u32[]{:S(2)}, u32[]{:S(2)}) collective-permute-start(bf16[2,256,128]{2,1,0:T(8,128)(2,1)S(1)} %get-tuple-element.34.refs_0_), channel_id=1, source_target_pairs={{0,4},{4,8},{8,12},{1,5},{5,9},{9,13},{2,6},{6,10},{10,14},{3,7},{... | collective-permute-start | bytes 393224 | tf_op jit(solution)/shard_map/ppermute | solution.py:25
  11.7 1.3 %collective-permute-start.1 = (bf16[2,256,128]{2,1,0:T(8,128)(2,1)S(1)}, bf16[2,256,128]{2,1,0:T(8,128)(2,1)S(1)}, u32[]{:S(2)}, u32[]{:S(2)}) collective-permute-start(bf16[2,256,128]{2,1,0:T(8,128)(2,1)S(1)} %get-tuple-element.34.refs_0_), channel_id=1, source_target_pairs={{0,8},{4,12},{1,9},{5,13},{2,10},{6,14},{3,11},{7,15},{16,24},{20,... | collective-permute-start | bytes 393224 | tf_op jit(solution)/shard_map/ppermute | solution.py:25
  13.1 0.0 copy-done
  13.1 0.0 copy-start.1
  13.1 1.0 %copy-done.1 = bf16[256,8,128]{2,1,0:T(8,128)(2,1)S(1)} copy-done((bf16[256,8,128]{2,1,0:T(8,128)(2,1)S(1)}, bf16[256,8,128]{2,1,0:T(8,128)(2,1)}, u32[]{:S(2)}) %copy-start.1) | copy-done | bytes 524312
  14.1 0.5 shard_map.84
  14.6 0.0 collective-permute-done.3.refs_1_
  14.6 0.7 %collective-permute-start.2 = (bf16[2,256,128]{2,1,0:T(8,128)(2,1)S(1)}, bf16[2,256,128]{2,1,0:T(8,128)(2,1)S(1)}, u32[]{:S(2)}, u32[]{:S(2)}) collective-permute-start(bf16[2,256,128]{2,1,0:T(8,128)(2,1)S(1)} %get-tuple-element.34.refs_0_), channel_id=1, source_target_pairs={{0,12},{1,13},{2,14},{3,15},{16,28},{17,29},{18,30},{19,31}} | collective-permute-start | bytes 393224 | tf_op jit(solution)/shard_map/ppermute | solution.py:25
  15.3 1.2 %collective-permute-done.4.refs_2_ = bf16[2,256,128]{2,1,0:T(8,128)(2,1)S(1)} collective-permute-done((bf16[2,256,128]{2,1,0:T(8,128)(2,1)S(1)}, bf16[2,256,128]{2,1,0:T(8,128)(2,1)S(1)}, u32[]{:S(2)}, u32[]{:S(2)}) %collective-permute-start.4) | collective-permute-done | bytes 131104 | tf_op jit(solution)/shard_map/ppermute | solution.py:25
  16.5 0.0 collective-permute-done.5.refs_3_
  16.5 0.0 copy-start.4
  16.5 0.7 %copy-done.4 = s32[2,17]{1,0:T(2,128)S(1)} copy-done((s32[2,17]{1,0:T(2,128)S(1)}, s32[2,17]{1,0:T(2,128)}, u32[]{:S(2)}) %copy-start.4) | copy-done | bytes 160
  17.2 4.8 %shard_map.87 = (bf16[1024,128]{1,0:T(8,128)(2,1)S(1)}, bf16[1024,128]{1,0:T(8,128)(2,1)S(1)}, f32[2,256,128]{2,1,0:T(8,128)S(1)}, bf16[2,256,128]{2,1,0:T(8,128...) custom-call(s32[2]{0:T(128)S(1)} %pad_add_fusion.meta, s32[2,17]{1,0:T(2,128)S(1)} %copy-done.4, ...), custom_call_target="tpu_custom_call" | custom-call | flops 1610612736 | bytes 1048576 | tf_op jit(solution)/shard_map/pallas_call | solution.py:229
  22.0 1.3 %collective-permute-start.10 = (bf16[2,256,128]{2,1,0:T(8,128)(2,1)S(1)}, bf16[2,256,128]{2,1,0:T(8,128)(2,1)S(1)}, u32[]{:S(2)}, u32[]{:S(2)}) collective-permute-start(bf16[2,256,128]{2,1,0:T(8,128)(2,1)S(1)} %get-tuple-element.52), channel_id=1, source_target_pairs={{8,0},{12,4},{9,1},{13,5},{10,2},{14,6},{11,3},{15,7},{24,16},{28,... | collective-permute-start | bytes 393224 | tf_op jit(solution)/shard_map/ppermute | solution.py:25
  23.3 1.9 %collective-permute-start.11 = (bf16[2,256,128]{2,1,0:T(8,128)(2,1)S(1)}, bf16[2,256,128]{2,1,0:T(8,128)(2,1)S(1)}, u32[]{:S(2)}, u32[]{:S(2)}) collective-permute-start(bf16[2,256,128]{2,1,0:T(8,128)(2,1)S(1)} %get-tuple-element.53), channel_id=1, source_target_pairs={{4,0},{8,4},{12,8},{5,1},{9,5},{13,9},{6,2},{10,6},{14,10},{7,3},{... | collective-permute-start | bytes 393224 | tf_op jit(solution)/shard_map/ppermute | solution.py:25
  25.2 0.7 %collective-permute-done.refs_1_ = bf16[2,256,128]{2,1,0:T(8,128)(2,1)S(1)} collective-permute-done((bf16[2,256,128]{2,1,0:T(8,128)(2,1)S(1)}, bf16[2,256,128]{2,1,0:T(8,128)(2,1)S(1)}, u32[]{:S(2)}, u32[]{:S(2)}) %collective-permute-start) | collective-permute-done | bytes 131104 | tf_op jit(solution)/shard_map/ppermute | solution.py:25
  25.9 0.7 %collective-permute-start.9 = (bf16[2,256,128]{2,1,0:T(8,128)(2,1)S(1)}, bf16[2,256,128]{2,1,0:T(8,128)(2,1)S(1)}, u32[]{:S(2)}, u32[]{:S(2)}) collective-permute-start(bf16[2,256,128]{2,1,0:T(8,128)(2,1)S(1)} %get-tuple-element.51), channel_id=1, source_target_pairs={{12,0},{13,1},{14,2},{15,3},{28,16},{29,17},{30,18},{31,19}} | collective-permute-start | bytes 393224 | tf_op jit(solution)/shard_map/ppermute | solution.py:25
  26.6 2.3 %collective-permute-done.1.refs_2_ = bf16[2,256,128]{2,1,0:T(8,128)(2,1)S(1)} collective-permute-done((bf16[2,256,128]{2,1,0:T(8,128)(2,1)S(1)}, bf16[2,256,128]{2,1,0:T(8,128)(2,1)S(1)}, u32[]{:S(2)}, u32[]{:S(2)}) %collective-permute-start.1) | collective-permute-done | bytes 131104 | tf_op jit(solution)/shard_map/ppermute | solution.py:25
  28.9 0.0 collective-permute-done.2.refs_3_
  28.9 5.0 %shard_map.86 = (bf16[1024,128]{1,0:T(8,128)(2,1)S(1)}, bf16[1024,128]{1,0:T(8,128)(2,1)S(1)}, f32[2,256,128]{2,1,0:T(8,128)S(1)}, bf16[2,256,128]{2,1,0:T(8,128...) custom-call(s32[2]{0:T(128)S(1)} %pad_add_fusion.meta, s32[2,17]{1,0:T(2,128)S(1)} %copy-done.4, ...), custom_call_target="tpu_custom_call" | custom-call | flops 1610612736 | bytes 1048576 | tf_op jit(solution)/shard_map/pallas_call | solution.py:229
  33.8 0.7 %collective-permute-start.6 = (bf16[2,256,128]{2,1,0:T(8,128)(2,1)S(1)}, bf16[2,256,128]{2,1,0:T(8,128)(2,1)S(1)}, u32[]{:S(2)}, u32[]{:S(2)}) collective-permute-start(bf16[2,256,128]{2,1,0:T(8,128)(2,1)S(1)} %get-tuple-element.47), channel_id=1, source_target_pairs={{12,0},{13,1},{14,2},{15,3},{28,16},{29,17},{30,18},{31,19}} | collective-permute-start | bytes 393224 | tf_op jit(solution)/shard_map/ppermute | solution.py:25
  34.5 1.3 %collective-permute-start.7 = (bf16[2,256,128]{2,1,0:T(8,128)(2,1)S(1)}, bf16[2,256,128]{2,1,0:T(8,128)(2,1)S(1)}, u32[]{:S(2)}, u32[]{:S(2)}) collective-permute-start(bf16[2,256,128]{2,1,0:T(8,128)(2,1)S(1)} %get-tuple-element.48), channel_id=1, source_target_pairs={{8,0},{12,4},{9,1},{13,5},{10,2},{14,6},{11,3},{15,7},{24,16},{28,... | collective-permute-start | bytes 393224 | tf_op jit(solution)/shard_map/ppermute | solution.py:25
  35.8 0.0 collective-permute-done.10
  35.8 1.9 %collective-permute-start.8 = (bf16[2,256,128]{2,1,0:T(8,128)(2,1)S(1)}, bf16[2,256,128]{2,1,0:T(8,128)(2,1)S(1)}, u32[]{:S(2)}, u32[]{:S(2)}) collective-permute-start(bf16[2,256,128]{2,1,0:T(8,128)(2,1)S(1)} %get-tuple-element.49), channel_id=1, source_target_pairs={{4,0},{8,4},{12,8},{5,1},{9,5},{13,9},{6,2},{10,6},{14,10},{7,3},{... | collective-permute-start | bytes 393224 | tf_op jit(solution)/shard_map/ppermute | solution.py:25
  37.8 0.0 collective-permute-done.11
  37.8 0.0 collective-permute-done.9
  37.8 0.1 add_convert_fusion.refs_1_
  37.9 2.4 %collective-permute-start.13 = (bf16[2,256,128]{2,1,0:T(8,128)(2,1)S(1)}, bf16[2,256,128]{2,1,0:T(8,128)(2,1)S(1)}, u32[]{:S(2)}, u32[]{:S(2)}) collective-permute-start(bf16[2,256,128]{2,1,0:T(8,128)(2,1)S(1)} %add_convert_fusion.refs_1_), channel_id=1, source_target_pairs={{0,1},{1,0},{2,3},{3,2},{4,5},{5,4},{6,7},{7,6},{8,9},{9,8},{10,11... | collective-permute-start | bytes 393224 | tf_op jit(solution)/shard_map/ppermute | solution.py:257
  40.3 0.0 collective-permute-done.6
  40.3 7.5 %collective-permute-done.7 = bf16[2,256,128]{2,1,0:T(8,128)(2,1)S(1)} collective-permute-done((bf16[2,256,128]{2,1,0:T(8,128)(2,1)S(1)}, bf16[2,256,128]{2,1,0:T(8,128)(2,1)S(1)}, u32[]{:S(2)}, u32[]{:S(2)}) %collective-permute-start.7) | collective-permute-done | bytes 131104 | tf_op jit(solution)/shard_map/ppermute | solution.py:25
  47.7 0.7 %collective-permute-done.8 = bf16[2,256,128]{2,1,0:T(8,128)(2,1)S(1)} collective-permute-done((bf16[2,256,128]{2,1,0:T(8,128)(2,1)S(1)}, bf16[2,256,128]{2,1,0:T(8,128)(2,1)S(1)}, u32[]{:S(2)}, u32[]{:S(2)}) %collective-permute-start.8) | collective-permute-done | bytes 131104 | tf_op jit(solution)/shard_map/ppermute | solution.py:25
  48.4 0.1 add_convert_fusion.1.refs_0_
  48.5 4.2 %collective-permute-start.12 = (bf16[2,256,128]{2,1,0:T(8,128)(2,1)S(1)}, bf16[2,256,128]{2,1,0:T(8,128)(2,1)S(1)}, u32[]{:S(2)}, u32[]{:S(2)}) collective-permute-start(bf16[2,256,128]{2,1,0:T(8,128)(2,1)S(1)} %add_convert_fusion.1.refs_0_), channel_id=1, source_target_pairs={{0,1},{1,0},{2,3},{3,2},{4,5},{5,4},{6,7},{7,6},{8,9},{9,8},{10,11... | collective-permute-start | bytes 393224 | tf_op jit(solution)/shard_map/ppermute | solution.py:257
  52.7 1.5 %shard_map.88 = (bf16[2048,128]{1,0:T(8,128)(2,1)}, bf16[2048,128]{1,0:T(8,128)(2,1)}) custom-call(bf16[1024,128]{1,0:T(8,128)(2,1)S(1)} %get-tuple-element.35.refs_0_, bf16[1024,128]{1,0:T(8,128)(2,1)S(1)} %get-tuple-element.36.refs_1_, bf16[1024,128]{1,0:T(8,128)(2,1)S(1)} %get-tuple-element.42.refs_2_, bf16[1024,128]{1,0:T(8,128)(2,1)S(1)} %get-tuple-element.43.refs_3_), custom_call_target="tpu_custom_call" | custom-call | bytes 1048576 | tf_op jit(solution)/shard_map/pallas_call | solution.py:251
  54.2 0.0 collective-permute-done.13.refs_3_
  54.2 0.0 collective-permute-done.12.refs_2_
  54.2 1.5 %shard_map.89 = (bf16[1024,128]{1,0:T(8,128)(2,1)}, bf16[1024,128]{1,0:T(8,128)(2,1)}) custom-call(s32[2]{0:T(128)S(1)} %pad_add_fusion.meta, bf16[2,256,128]{2,1,0:T(8,128)(2,1)S(1)} %add_convert_fusion.1.refs_0_, bf16[2,256,128]{2,1,0:T(8,128)(2,1)S(1)} %add_convert_fusion.refs_1_, bf16[2,256,128]{2,1,0:T(8,128)(2,1)S(1)} %collective-permute-done.12.refs_2_, ...), custom_call_target="tpu_custom_call" | custom-call | bytes 1048576 | tf_op jit(solution)/shard_map/pallas_call | solution.py:258
Async XLA Ops:
  0.6 12.4 %copy-start = (bf16[256,8,128]{2,1,0:T(8,128)(2,1)S(1)}, bf16[256,8,128]{2,1,0:T(8,128)(2,1)}, u32[]{:S(2)}) copy-start(bf16[256,8,128]{2,1,0:T(8,128)(2,1)} %param.5) | copy-start | bytes 1572868
  0.7 1.0 %copy-start.2 = (bf16[256,4,128]{2,1,0:T(4,128)(2,1)S(1)}, bf16[256,4,128]{2,1,0:T(4,128)(2,1)}, u32[]{:S(2)}) copy-start(bf16[256,4,128]{2,1,0:T(4,128)(2,1)} %param.6) | copy-start | bytes 786436
  1.7 0.9 %copy-start.3 = (bf16[256,4,128]{2,1,0:T(4,128)(2,1)S(1)}, bf16[256,4,128]{2,1,0:T(4,128)(2,1)}, u32[]{:S(2)}) copy-start(bf16[256,4,128]{2,1,0:T(4,128)(2,1)} %param.7) | copy-start | bytes 786436
  3.3 11.3 %collective-permute-start.3 = (bf16[2,256,128]{2,1,0:T(8,128)(2,1)S(1)}, bf16[2,256,128]{2,1,0:T(8,128)(2,1)S(1)}, u32[]{:S(2)}, u32[]{:S(2)}) collective-permute-start(bf16[2,256,128]{2,1,0:T(8,128)(2,1)S(1)} %get-tuple-element.41.refs_0_), channel_id=1, source_target_pairs={{0,4},{4,8},{8,12},{1,5},{5,9},{9,13},{2,6},{6,10},{10,14},{3,7},{... | collective-permute-start | bytes 393224 | tf_op jit(solution)/shard_map/ppermute | solution.py:25
  6.6 9.9 %collective-permute-start.4 = (bf16[2,256,128]{2,1,0:T(8,128)(2,1)S(1)}, bf16[2,256,128]{2,1,0:T(8,128)(2,1)S(1)}, u32[]{:S(2)}, u32[]{:S(2)}) collective-permute-start(bf16[2,256,128]{2,1,0:T(8,128)(2,1)S(1)} %get-tuple-element.41.refs_0_), channel_id=1, source_target_pairs={{0,8},{4,12},{1,9},{5,13},{2,10},{6,14},{3,11},{7,15},{16,24},{20,... | collective-permute-start | bytes 393224 | tf_op jit(solution)/shard_map/ppermute | solution.py:25
  8.9 7.6 %collective-permute-start.5 = (bf16[2,256,128]{2,1,0:T(8,128)(2,1)S(1)}, bf16[2,256,128]{2,1,0:T(8,128)(2,1)S(1)}, u32[]{:S(2)}, u32[]{:S(2)}) collective-permute-start(bf16[2,256,128]{2,1,0:T(8,128)(2,1)S(1)} %get-tuple-element.41.refs_0_), channel_id=1, source_target_pairs={{0,12},{1,13},{2,14},{3,15},{16,28},{17,29},{18,30},{19,31}} | collective-permute-start | bytes 393224 | tf_op jit(solution)/shard_map/ppermute | solution.py:25
  9.6 16.4 %collective-permute-start = (bf16[2,256,128]{2,1,0:T(8,128)(2,1)S(1)}, bf16[2,256,128]{2,1,0:T(8,128)(2,1)S(1)}, u32[]{:S(2)}, u32[]{:S(2)}) collective-permute-start(bf16[2,256,128]{2,1,0:T(8,128)(2,1)S(1)} %get-tuple-element.34.refs_0_), channel_id=1, source_target_pairs={{0,4},{4,8},{8,12},{1,5},{5,9},{9,13},{2,6},{6,10},{10,14},{3,7},{... | collective-permute-start | bytes 393224 | tf_op jit(solution)/shard_map/ppermute | solution.py:25
  11.7 17.1 %collective-permute-start.1 = (bf16[2,256,128]{2,1,0:T(8,128)(2,1)S(1)}, bf16[2,256,128]{2,1,0:T(8,128)(2,1)S(1)}, u32[]{:S(2)}, u32[]{:S(2)}) collective-permute-start(bf16[2,256,128]{2,1,0:T(8,128)(2,1)S(1)} %get-tuple-element.34.refs_0_), channel_id=1, source_target_pairs={{0,8},{4,12},{1,9},{5,13},{2,10},{6,14},{3,11},{7,15},{16,24},{20,... | collective-permute-start | bytes 393224 | tf_op jit(solution)/shard_map/ppermute | solution.py:25
  13.1 1.0 %copy-start.1 = (bf16[256,8,128]{2,1,0:T(8,128)(2,1)S(1)}, bf16[256,8,128]{2,1,0:T(8,128)(2,1)}, u32[]{:S(2)}) copy-start(bf16[256,8,128]{2,1,0:T(8,128)(2,1)} %param.8) | copy-start | bytes 1572868
  14.6 14.2 %collective-permute-start.2 = (bf16[2,256,128]{2,1,0:T(8,128)(2,1)S(1)}, bf16[2,256,128]{2,1,0:T(8,128)(2,1)S(1)}, u32[]{:S(2)}, u32[]{:S(2)}) collective-permute-start(bf16[2,256,128]{2,1,0:T(8,128)(2,1)S(1)} %get-tuple-element.34.refs_0_), channel_id=1, source_target_pairs={{0,12},{1,13},{2,14},{3,15},{16,28},{17,29},{18,30},{19,31}} | collective-permute-start | bytes 393224 | tf_op jit(solution)/shard_map/ppermute | solution.py:25
  16.5 0.7 %copy-start.4 = (s32[2,17]{1,0:T(2,128)S(1)}, s32[2,17]{1,0:T(2,128)}, u32[]{:S(2)}) copy-start(s32[2,17]{1,0:T(2,128)} %mask.3) | copy-start | bytes 412
  22.0 13.8 %collective-permute-start.10 = (bf16[2,256,128]{2,1,0:T(8,128)(2,1)S(1)}, bf16[2,256,128]{2,1,0:T(8,128)(2,1)S(1)}, u32[]{:S(2)}, u32[]{:S(2)}) collective-permute-start(bf16[2,256,128]{2,1,0:T(8,128)(2,1)S(1)} %get-tuple-element.52), channel_id=1, source_target_pairs={{8,0},{12,4},{9,1},{13,5},{10,2},{14,6},{11,3},{15,7},{24,16},{28,... | collective-permute-start | bytes 393224 | tf_op jit(solution)/shard_map/ppermute | solution.py:25
  23.3 14.5 %collective-permute-start.11 = (bf16[2,256,128]{2,1,0:T(8,128)(2,1)S(1)}, bf16[2,256,128]{2,1,0:T(8,128)(2,1)S(1)}, u32[]{:S(2)}, u32[]{:S(2)}) collective-permute-start(bf16[2,256,128]{2,1,0:T(8,128)(2,1)S(1)} %get-tuple-element.53), channel_id=1, source_target_pairs={{4,0},{8,4},{12,8},{5,1},{9,5},{13,9},{6,2},{10,6},{14,10},{7,3},{... | collective-permute-start | bytes 393224 | tf_op jit(solution)/shard_map/ppermute | solution.py:25
  25.9 11.9 %collective-permute-start.9 = (bf16[2,256,128]{2,1,0:T(8,128)(2,1)S(1)}, bf16[2,256,128]{2,1,0:T(8,128)(2,1)S(1)}, u32[]{:S(2)}, u32[]{:S(2)}) collective-permute-start(bf16[2,256,128]{2,1,0:T(8,128)(2,1)S(1)} %get-tuple-element.51), channel_id=1, source_target_pairs={{12,0},{13,1},{14,2},{15,3},{28,16},{29,17},{30,18},{31,19}} | collective-permute-start | bytes 393224 | tf_op jit(solution)/shard_map/ppermute | solution.py:25
  33.8 6.4 %collective-permute-start.6 = (bf16[2,256,128]{2,1,0:T(8,128)(2,1)S(1)}, bf16[2,256,128]{2,1,0:T(8,128)(2,1)S(1)}, u32[]{:S(2)}, u32[]{:S(2)}) collective-permute-start(bf16[2,256,128]{2,1,0:T(8,128)(2,1)S(1)} %get-tuple-element.47), channel_id=1, source_target_pairs={{12,0},{13,1},{14,2},{15,3},{28,16},{29,17},{30,18},{31,19}} | collective-permute-start | bytes 393224 | tf_op jit(solution)/shard_map/ppermute | solution.py:25
  34.5 13.2 %collective-permute-start.7 = (bf16[2,256,128]{2,1,0:T(8,128)(2,1)S(1)}, bf16[2,256,128]{2,1,0:T(8,128)(2,1)S(1)}, u32[]{:S(2)}, u32[]{:S(2)}) collective-permute-start(bf16[2,256,128]{2,1,0:T(8,128)(2,1)S(1)} %get-tuple-element.48), channel_id=1, source_target_pairs={{8,0},{12,4},{9,1},{13,5},{10,2},{14,6},{11,3},{15,7},{24,16},{28,... | collective-permute-start | bytes 393224 | tf_op jit(solution)/shard_map/ppermute | solution.py:25
  35.8 12.6 %collective-permute-start.8 = (bf16[2,256,128]{2,1,0:T(8,128)(2,1)S(1)}, bf16[2,256,128]{2,1,0:T(8,128)(2,1)S(1)}, u32[]{:S(2)}, u32[]{:S(2)}) collective-permute-start(bf16[2,256,128]{2,1,0:T(8,128)(2,1)S(1)} %get-tuple-element.49), channel_id=1, source_target_pairs={{4,0},{8,4},{12,8},{5,1},{9,5},{13,9},{6,2},{10,6},{14,10},{7,3},{... | collective-permute-start | bytes 393224 | tf_op jit(solution)/shard_map/ppermute | solution.py:25
  37.9 16.3 %collective-permute-start.13 = (bf16[2,256,128]{2,1,0:T(8,128)(2,1)S(1)}, bf16[2,256,128]{2,1,0:T(8,128)(2,1)S(1)}, u32[]{:S(2)}, u32[]{:S(2)}) collective-permute-start(bf16[2,256,128]{2,1,0:T(8,128)(2,1)S(1)} %add_convert_fusion.refs_1_), channel_id=1, source_target_pairs={{0,1},{1,0},{2,3},{3,2},{4,5},{5,4},{6,7},{7,6},{8,9},{9,8},{10,11... | collective-permute-start | bytes 393224 | tf_op jit(solution)/shard_map/ppermute | solution.py:257
  48.5 5.7 %collective-permute-start.12 = (bf16[2,256,128]{2,1,0:T(8,128)(2,1)S(1)}, bf16[2,256,128]{2,1,0:T(8,128)(2,1)S(1)}, u32[]{:S(2)}, u32[]{:S(2)}) collective-permute-start(bf16[2,256,128]{2,1,0:T(8,128)(2,1)S(1)} %add_convert_fusion.1.refs_0_), channel_id=1, source_target_pairs={{0,1},{1,0},{2,3},{3,2},{4,5},{5,4},{6,7},{7,6},{8,9},{9,8},{10,11... | collective-permute-start | bytes 393224 | tf_op jit(solution)/shard_map/ppermute | solution.py:257

commit v2 on v1

v2 whole, which is shorter than its diff:
```python
import functools
import math

import jax
import jax.numpy as jnp
from jax import lax
from jax.experimental import pallas as pl
from jax.experimental.pallas import tpu as pltpu
from jax.sharding import PartitionSpec as P

HEADS = 32
KV_HEADS = 8
BLOCK = 128
WINDOW = 2048
NEGATIVE = -1e30
LOG2E = 1.4426950408889634

VMEM = pl.BlockSpec(memory_space=pltpu.VMEM)
SMEM = pl.BlockSpec(memory_space=pltpu.SMEM)
HBM = pl.BlockSpec(memory_space=pltpu.HBM)


def shifted(value, axis, steps):
    count = lax.axis_size(axis)
    first, last = (max(0, -steps), min(count, count - steps))
    return lax.ppermute(value, axis, [(source, source + steps) for source in range(first, last)])


def after(value, *others):
    return lax.optimization_barrier((value, *others))[0]


def dot(left, right):
    return jnp.dot(left, right, preferred_element_type=jnp.float32)


def pack_kernel(rows, kv_heads, used, meta, key_in, value_in, *refs):
    outs, (low, wide, sems) = (refs[:used], refs[used:])
    copies = [
        pltpu.make_async_copy(source, low.at[place], sems.at[place])
        for place, source in enumerate((key_in, value_in))
    ]
    for copy in copies:
        copy.start()
    for place, copy in enumerate(copies):
        copy.wait()
        wide[...] = low[place].astype(jnp.float32)
        for head in range(used):
            picked = wide[pl.ds(meta[1] + head, rows, stride=kv_heads), :]
            outs[head][place] = picked.astype(jnp.bfloat16)


def turn_kernel(rows, q_heads, used, query_in, grad_in, *refs):
    outs, wide = (refs[: 4 * used], refs[4 * used])
    per = q_heads // used
    for place, source in enumerate((query_in, grad_in)):
        wide[...] = source[...].astype(jnp.float32)
        for head in range(q_heads):
            picked = wide[pl.ds(head, rows, stride=q_heads), :]
            slot, local = divmod(head, per)
            straight, flipped = outs[4 * slot + 2 * place : 4 * slot + 2 * place + 2]
            straight[pl.ds(local * rows, rows), :] = picked.astype(jnp.bfloat16)
            flipped[:, pl.ds(local * rows, rows)] = picked.T.astype(jnp.bfloat16)


def attend_part(count, rows, per, lags, offsets, meta, q_ref, qt_ref, g_ref, gt_ref, *refs):
    pairs = refs[:lags]
    out_ref, qgrad_ref, own_ref = refs[lags : lags + 3]
    terms = refs[lags + 3 : 2 * lags + 2]
    powers, low_tile, tops, sums, out_t, qgrad_t = refs[2 * lags + 2 :]
    shard = meta[0]
    blocks = rows // BLOCK
    head_size = q_ref.shape[1]
    scale = 1.0 / math.sqrt(head_size)
    to_exp2 = scale * LOG2E

    def each_lag(step):
        if count is None:
            step(0)
            for lag in range(1, lags):
                pl.when(shard >= lag)(functools.partial(step, lag))
        else:
            for lag in range(count):
                step(lag)

    def columns(head):
        return slice(head * rows, (head + 1) * rows)

    def fold(op, tile):
        return op(op(tile.reshape(-1, 8, tile.shape[1]), axis=0), axis=0, keepdims=True)

    tops[...] = jnp.full(tops.shape, NEGATIVE, jnp.float32)
    sums[...] = jnp.zeros(sums.shape, jnp.float32)
    out_t[...] = jnp.zeros(out_t.shape, jnp.float32)
    qgrad_t[...] = jnp.zeros(qgrad_t.shape, jnp.float32)

    def score_step(lag):
        query_pos = lax.broadcasted_iota(jnp.int32, (BLOCK, rows), 1)
        key_pos = lax.broadcasted_iota(jnp.int32, (BLOCK, rows), 0)
        query_block = lax.broadcasted_iota(jnp.int32, (1, rows), 1) // BLOCK
        for head in range(per):
            both = dot(pairs[lag][0], qt_ref[:, columns(head)])
            for block in range(blocks):
                tile = both[block * BLOCK : (block + 1) * BLOCK]
                gap = query_pos - key_pos + (lag * rows - block * BLOCK)
                if lag == 0:
                    tile = jnp.where(gap >= 0, tile, NEGATIVE)
                if (lag + 1) * rows > WINDOW:
                    tile = jnp.where(gap < WINDOW, tile, NEGATIVE)
                top = fold(jnp.max, tile)
                power = jnp.exp2((tile - top) * to_exp2)
                powers[lag, block * BLOCK : (block + 1) * BLOCK, columns(head)] = power
                shown = jnp.zeros((1, rows), jnp.int32)
                for seen in range(blocks):
                    distance = lag * blocks + seen - block
                    if 0 <= distance < offsets:
                        shown = jnp.where(query_block == seen, meta[2 + seen * offsets + distance], shown)
                place = lag * blocks + block
                tops[place : place + 1, columns(head)] = jnp.where(shown > 0, top, NEGATIVE)
                sums[place : place + 1, columns(head)] = fold(jnp.sum, power)

    each_lag(score_step)
    top = jnp.max(tops[...], axis=0, keepdims=True)
    factor = jnp.exp2((tops[...] - top) * to_exp2)
    tops[...] = factor / jnp.sum(factor * sums[...], axis=0, keepdims=True)

    def weigh(lag, head):
        tiles = []
        for block in range(blocks):
            place = lag * blocks + block
            power = powers[lag, block * BLOCK : (block + 1) * BLOCK, columns(head)]
            tiles.append(power * tops[place : place + 1, columns(head)])
        return jnp.concatenate(tiles, 0)

    def value_step(lag):
        value_t = pairs[lag][1].T
        for head in range(per):
            low = weigh(lag, head).astype(jnp.bfloat16)
            low_tile[lag, :, columns(head)] = low
            out_t[:, columns(head)] += dot(value_t, low)
        part = dot(low_tile[lag], g_ref[...])
        if lag == 0:
            own_ref[1] = part
        else:
            terms[lag - 1][1] = part.astype(jnp.bfloat16)

    each_lag(value_step)
    attended_t = out_t[...].astype(jnp.bfloat16).astype(jnp.float32)
    drift = jnp.sum(attended_t * gt_ref[...].astype(jnp.float32), axis=0, keepdims=True)
    out_ref[...] = attended_t.T.astype(jnp.bfloat16)

    def push_step(lag):
        for head in range(per):
            pushed = dot(pairs[lag][1], gt_ref[:, columns(head)])
            low = (weigh(lag, head) * (pushed - drift[:, columns(head)])).astype(jnp.bfloat16)
            low_tile[lag, :, columns(head)] = low

    each_lag(push_step)

    def slope_step(lag):
        key_t = pairs[lag][0].T
        qgrad_t[...] += dot(key_t, low_tile[lag])
        part = dot(low_tile[lag], q_ref[...]) * scale
        if lag == 0:
            own_ref[0] = part
        else:
            terms[lag - 1][0] = part.astype(jnp.bfloat16)

    each_lag(slope_step)
    qgrad_ref[...] = (qgrad_t[...] * scale).T.astype(jnp.bfloat16)


def attend_kernel(rows, per, lags, offsets, meta, *refs):
    if lags > 4:
        attend_part(None, rows, per, lags, offsets, meta, *refs)
        return
    there = jnp.minimum(meta[0] + 1, lags)
    for count in range(1, lags + 1):
        part = functools.partial(attend_part, count, rows, per, lags, offsets)
        pl.when(there == count)(functools.partial(part, meta, *refs))


def unturn_kernel(rows, q_heads, used, *refs):
    sources, outs, wide = (refs[: 2 * used], refs[2 * used : 2 * used + 2], refs[-1])
    per = q_heads // used
    for place, target in enumerate(outs):
        for head in range(q_heads):
            slot, local = divmod(head, per)
            tile = sources[2 * slot + place][pl.ds(local * rows, rows), :]
            wide[pl.ds(head, rows, stride=q_heads), :] = tile.astype(jnp.float32)
        target[...] = wide[...].astype(jnp.bfloat16)


def join_kernel(rows, kv_heads, used, meta, *refs):
    own, other = (refs[:used], refs[used : 2 * used])
    outs, wide = (refs[2 * used : 2 * used + 2], refs[-1])
    first = meta[1]
    for place, target in enumerate(outs):
        for head in range(used):
            mine = own[head][place].astype(jnp.float32)
            theirs = other[head][place].astype(jnp.float32)
            if used == kv_heads:
                wide[pl.ds(head, rows, stride=kv_heads), :] = mine + theirs
            else:
                away = kv_heads - used - first
                wide[pl.ds(first + head, rows, stride=kv_heads), :] = mine
                wide[pl.ds(away + head, rows, stride=kv_heads), :] = theirs
        target[...] = wide[...].astype(jnp.bfloat16)


def body(query, key_states, value_states, grad_out, block_mask):
    rows, q_heads, head_size = query.shape
    kv_heads = key_states.shape[1]
    lags = min(WINDOW // rows, lax.axis_size("seq") - 1) + 1
    used = max(1, q_heads * KV_HEADS // HEADS)
    per = q_heads // used
    width = per * rows
    low, wide = (jnp.bfloat16, jnp.float32)
    core_first = lax.axis_index("sub") * q_heads * KV_HEADS // HEADS
    shard = lax.axis_index("seq")
    meta = jnp.stack([shard, core_first]).astype(jnp.int32)

    def call(kernel, ins, outs, scratch, flops=0, moved=2**20, limit=28):
        return pl.pallas_call(
            kernel,
            in_specs=ins,
            out_specs=[VMEM] * len(outs),
            out_shape=[jax.ShapeDtypeStruct(*o) for o in outs],
            scratch_shapes=[pltpu.VMEM(*s) if isinstance(s, tuple) else s for s in scratch],
            compiler_params=pltpu.CompilerParams(vmem_limit_bytes=limit * 2**20),
            cost_estimate=pl.CostEstimate(flops=flops, bytes_accessed=moved, transcendentals=0),
        )

    packed = call(
        functools.partial(pack_kernel, rows, kv_heads, used),
        [SMEM, HBM, HBM],
        [((2, rows, head_size), low)] * used,
        [
            ((2, rows * kv_heads, head_size), low),
            ((rows * kv_heads, head_size), wide),
            pltpu.SemaphoreType.DMA((2,)),
        ],
        limit=28,
    )(meta, key_states.reshape(-1, head_size), value_states.reshape(-1, head_size))
    turned = call(
        functools.partial(turn_kernel, rows, q_heads, used),
        [VMEM, VMEM],
        [((width, head_size), low), ((head_size, width), low)] * (2 * used),
        [((rows * q_heads, head_size), wide)],
    )(query.reshape(-1, head_size), grad_out.reshape(-1, head_size))
    full_meta = jnp.concatenate([meta, after(block_mask, *packed).reshape(-1)])

    results, sums = ([], [])
    for head in range(used):
        pairs = [packed[head]] + [shifted(packed[head], "seq", lag) for lag in range(1, lags)]
        attended, qgrad, own, *terms = call(
            functools.partial(attend_kernel, rows, per, lags, block_mask.shape[1]),
            [SMEM] + [VMEM] * (4 + lags),
            [((width, head_size), low)] * 2
            + [((2, rows, head_size), wide)]
            + [((2, rows, head_size), low)] * (lags - 1),
            [
                ((lags, rows, width), wide),
                ((lags, rows, width), low),
                ((lags * (rows // BLOCK), width), wide),
                ((lags * (rows // BLOCK), width), wide),
                ((head_size, width), wide),
                ((head_size, width), wide),
            ],
            flops=12 * lags * rows * width * head_size,
        )(full_meta, *turned[4 * head : 4 * head + 4], *pairs)
        results += [attended, qgrad]
        for lag in range(lags - 1, 0, -1):
            own = own + shifted(terms[lag - 1], "seq", -lag).astype(wide)
        sums.append(own.astype(low))

    attended, qgrad = call(
        functools.partial(unturn_kernel, rows, q_heads, used),
        [VMEM] * (2 * used),
        [((rows * q_heads, head_size), low)] * 2,
        [((rows * q_heads, head_size), wide)],
    )(*results)
    others = [lax.ppermute(value, "sub", [(0, 1), (1, 0)]) for value in sums]
    key_grad, value_grad = call(
        functools.partial(join_kernel, rows, kv_heads, used),
        [SMEM] + [VMEM] * (2 * used),
        [((rows * kv_heads, head_size), low)] * 2,
        [((rows * kv_heads, head_size), wide)],
    )(meta, *sums, *others)
    return (
        attended.reshape(rows, q_heads, head_size),
        qgrad.reshape(rows, q_heads, head_size),
        key_grad.reshape(rows, kv_heads, head_size),
        value_grad.reshape(rows, kv_heads, head_size),
    )


def solution(mesh):
    q_spec = P(("groups", "seq"), ("tensor", "sub"), None)
    kv_spec = P(("groups", "seq"), "tensor", None)
    return jax.shard_map(
        body,
        mesh=mesh,
        in_specs=(q_spec, kv_spec, kv_spec, q_spec, P(("groups", "seq"), None)),
        out_specs=(q_spec, q_spec, kv_spec, kv_spec),
        check_vma=False,
    )
```

time: 56.6 us -> 51.7 us (0.913)
  Pallas kernels: 13.9 us -> 9.73 us
  waiting for transfers between devices: 12.3 us -> 16 us
  starting transfers between devices: 24.7 us -> 21.3 us
  local copies, waits for them, and re-layouts: 3.67 us -> 3.08 us
    pallas_call x3, Pallas kernels: 10.4 us -> 6.25 us  [the longest x2 5.54 us: body(): call(functools.partial(attend_kernel, rows, per, lags, block_mask.shape[1...]
    ppermute x2, starting transfers between devices: 6.65 us -> 2.59 us  [body(): others = [lax.ppermute(value, 'sub', [(0, 1), (1, 0)]) for value in sums]]
    ppermute x12, waiting for transfers between devices: 12.3 us -> 16 us  [shifted(): lax.ppermute(value, axis, [(source, source + steps) for source in range(f...]
    unnamed x10, local copies, waits for them, and re-layouts: 3.67 us -> 3 us
    ppermute x12, starting transfers between devices: 18.1 us -> 18.7 us  [shifted(): lax.ppermute(value, axis, [(source, source + steps) for source in range(f...]
  transfers between devices with their start and end apart: 14 -> 14, of which waited for: 5 -> 5; matrix products, arithmetic and copies ran while one was open for 0% -> 1% of each run, Pallas kernels for 21% -> 15%
where the time goes in v2:
time: 51.7 us; the launch traced here: 51.3 us
  starting transfers between devices  21.3 us (41%)
  waiting for transfers between devices  16 us (31%)
  Pallas kernels  9.73 us (19%)
  local copies, waits for them, and re-layouts  3.08 us (6%)
  between operations  0.84 us (2%)
    ppermute x12, starting transfers between devices, shifted(): lax.ppermute(value, axis, [(source, source + steps) for source in range(f...  18.7 us
    ppermute x12, waiting for transfers between devices, shifted(): lax.ppermute(value, axis, [(source, source + steps) for source in range(f...  16 us
    pallas_call x2, Pallas kernels, body(): call(functools.partial(attend_kernel, rows, per, lags, block_mask.shape[1...  5.54 us
    unnamed x10, local copies, waits for them, and re-layouts  3 us
    ppermute x2, starting transfers between devices, body(): others = [lax.ppermute(value, 'sub', [(0, 1), (1, 0)]) for value in sums]  2.59 us
    pallas_call x1, Pallas kernels, body(): call(functools.partial(join_kernel, rows, kv_heads, used), [SMEM] + [VMEM...  1.5 us
    pallas_call x1, Pallas kernels, body(): call(functools.partial(unturn_kernel, rows, q_heads, used), [VMEM] * (2 *...  1.47 us
  transfers between devices with their start and end apart: 14, of which 5 were waited for; matrix products, arithmetic and copies ran while one was open for 1% of the time, Pallas kernels for 15%

profile of v2, /device:TPU:13, one launch (start us, length us, event | category | flops | bytes accessed | tf_op | source)
XLA Modules:
  0.0 51.3 jit_solution(66815113789183635)
XLA Ops:
  0.6 0.0 copy-start
  0.7 0.1 pad_add_fusion.meta
  0.7 0.0 copy-start.2
  0.7 1.0 %copy-done.2 = bf16[256,4,128]{2,1,0:T(4,128)(2,1)S(1)} copy-done((bf16[256,4,128]{2,1,0:T(4,128)(2,1)S(1)}, bf16[256,4,128]{2,1,0:T(4,128)(2,1)}, u32[]{:S(2)}) %copy-start.2) | copy-done | bytes 262168
  1.7 0.0 copy-start.3
  1.7 0.9 %copy-done.3 = bf16[256,4,128]{2,1,0:T(4,128)(2,1)S(1)} copy-done((bf16[256,4,128]{2,1,0:T(4,128)(2,1)S(1)}, bf16[256,4,128]{2,1,0:T(4,128)(2,1)}, u32[]{:S(2)}) %copy-start.3) | copy-done | bytes 262168
  2.7 0.7 %shard_map.84 = (bf16[2,256,128]{2,1,0:T(8,128)(2,1)S(1)}, bf16[2,256,128]{2,1,0:T(8,128)(2,1)S(1)}) custom-call(s32[2]{0:T(128)S(1)} %pad_add_fusion.meta, bf16[1024,128]{1,0:T(8,128)(2,1)S(1)} %bitcast.12, bf16[1024,128]{1,0:T(8,128)(2,1)S(1)} %bitcast.13), custom_call_target="tpu_custom_call" | custom-call | bytes 1048576 | tf_op jit(solution)/shard_map/pallas_call | solution.py:234
  3.4 0.0 copy-start.4
  3.4 3.2 %collective-permute-start.3 = (bf16[2,256,128]{2,1,0:T(8,128)(2,1)S(1)}, bf16[2,256,128]{2,1,0:T(8,128)(2,1)S(1)}, u32[]{:S(2)}, u32[]{:S(2)}) collective-permute-start(bf16[2,256,128]{2,1,0:T(8,128)(2,1)S(1)} %get-tuple-element.32.refs_4_), channel_id=1, source_target_pairs={{0,4},{4,8},{8,12},{1,5},{5,9},{9,13},{2,6},{6,10},{10,14},{3,7},{... | collective-permute-start | bytes 393224 | tf_op jit(solution)/shard_map/ppermute | solution.py:26
  6.6 2.3 %collective-permute-start.4 = (bf16[2,256,128]{2,1,0:T(8,128)(2,1)S(1)}, bf16[2,256,128]{2,1,0:T(8,128)(2,1)S(1)}, u32[]{:S(2)}, u32[]{:S(2)}) collective-permute-start(bf16[2,256,128]{2,1,0:T(8,128)(2,1)S(1)} %get-tuple-element.32.refs_4_), channel_id=1, source_target_pairs={{0,8},{4,12},{1,9},{5,13},{2,10},{6,14},{3,11},{7,15},{16,24},{20,... | collective-permute-start | bytes 393224 | tf_op jit(solution)/shard_map/ppermute | solution.py:26
  8.9 0.7 %collective-permute-start.5 = (bf16[2,256,128]{2,1,0:T(8,128)(2,1)S(1)}, bf16[2,256,128]{2,1,0:T(8,128)(2,1)S(1)}, u32[]{:S(2)}, u32[]{:S(2)}) collective-permute-start(bf16[2,256,128]{2,1,0:T(8,128)(2,1)S(1)} %get-tuple-element.32.refs_4_), channel_id=1, source_target_pairs={{0,12},{1,13},{2,14},{3,15},{16,28},{17,29},{18,30},{19,31}} | collective-permute-start | bytes 393224 | tf_op jit(solution)/shard_map/ppermute | solution.py:26
  9.6 2.2 %collective-permute-start = (bf16[2,256,128]{2,1,0:T(8,128)(2,1)S(1)}, bf16[2,256,128]{2,1,0:T(8,128)(2,1)S(1)}, u32[]{:S(2)}, u32[]{:S(2)}) collective-permute-start(bf16[2,256,128]{2,1,0:T(8,128)(2,1)S(1)} %get-tuple-element.31.refs_4_), channel_id=1, source_target_pairs={{0,4},{4,8},{8,12},{1,5},{5,9},{9,13},{2,6},{6,10},{10,14},{3,7},{... | collective-permute-start | bytes 393224 | tf_op jit(solution)/shard_map/ppermute | solution.py:26
  11.8 1.3 %collective-permute-start.1 = (bf16[2,256,128]{2,1,0:T(8,128)(2,1)S(1)}, bf16[2,256,128]{2,1,0:T(8,128)(2,1)S(1)}, u32[]{:S(2)}, u32[]{:S(2)}) collective-permute-start(bf16[2,256,128]{2,1,0:T(8,128)(2,1)S(1)} %get-tuple-element.31.refs_4_), channel_id=1, source_target_pairs={{0,8},{4,12},{1,9},{5,13},{2,10},{6,14},{3,11},{7,15},{16,24},{20,... | collective-permute-start | bytes 393224 | tf_op jit(solution)/shard_map/ppermute | solution.py:26
  13.1 0.0 copy-done.4
  13.1 0.1 reshape.37
  13.2 0.0 copy-done
  13.2 0.0 copy-start.1
  13.2 1.0 %copy-done.1 = bf16[256,8,128]{2,1,0:T(8,128)(2,1)S(1)} copy-done((bf16[256,8,128]{2,1,0:T(8,128)(2,1)S(1)}, bf16[256,8,128]{2,1,0:T(8,128)(2,1)}, u32[]{:S(2)}) %copy-start.1) | copy-done | bytes 524312
  14.3 0.5 %shard_map.85 = (bf16[1024,128]{1,0:T(8,128)(2,1)S(1)}, bf16[128,1024]{1,0:T(8,128)(2,1)S(1)}, bf16[1024,128]{1,0:T(8,128)(2,1)S(1)}, bf16[128,1024]{1,0:T(8,128...) custom-call(bf16[2048,128]{1,0:T(8,128)(2,1)S(1)} %bitcast.10, ...), custom_call_target="tpu_custom_call" | custom-call | bytes 1048576 | tf_op jit(solution)/shard_map/pallas_call | solution.py:245
  14.8 0.1 pad_add_fusion.1.meta
  14.9 0.0 collective-permute-done.3.refs_5_
  14.9 0.7 %collective-permute-start.2 = (bf16[2,256,128]{2,1,0:T(8,128)(2,1)S(1)}, bf16[2,256,128]{2,1,0:T(8,128)(2,1)S(1)}, u32[]{:S(2)}, u32[]{:S(2)}) collective-permute-start(bf16[2,256,128]{2,1,0:T(8,128)(2,1)S(1)} %get-tuple-element.31.refs_4_), channel_id=1, source_target_pairs={{0,12},{1,13},{2,14},{3,15},{16,28},{17,29},{18,30},{19,31}} | collective-permute-start | bytes 393224 | tf_op jit(solution)/shard_map/ppermute | solution.py:26
  15.5 1.0 %collective-permute-done.4.refs_6_ = bf16[2,256,128]{2,1,0:T(8,128)(2,1)S(1)} collective-permute-done((bf16[2,256,128]{2,1,0:T(8,128)(2,1)S(1)}, bf16[2,256,128]{2,1,0:T(8,128)(2,1)S(1)}, u32[]{:S(2)}, u32[]{:S(2)}) %collective-permute-start.4) | collective-permute-done | bytes 131104 | tf_op jit(solution)/shard_map/ppermute | solution.py:26
  16.6 0.0 collective-permute-done.5.refs_7_
  16.6 2.7 %shard_map.87 = (bf16[1024,128]{1,0:T(8,128)(2,1)S(1)}, bf16[1024,128]{1,0:T(8,128)(2,1)S(1)}, f32[2,256,128]{2,1,0:T(8,128)S(1)}, bf16[2,256,128]{2,1,0:T(8,128...) custom-call(s32[36]{0:T(128)S(1)} %pad_add_fusion.1.meta, ...), custom_call_target="tpu_custom_call" | custom-call | flops 1610612736 | bytes 1048576 | tf_op jit(solution)/shard_map/pallas_call | solution.py:256
  19.2 1.3 %collective-permute-start.10 = (bf16[2,256,128]{2,1,0:T(8,128)(2,1)S(1)}, bf16[2,256,128]{2,1,0:T(8,128)(2,1)S(1)}, u32[]{:S(2)}, u32[]{:S(2)}) collective-permute-start(bf16[2,256,128]{2,1,0:T(8,128)(2,1)S(1)} %get-tuple-element.54), channel_id=1, source_target_pairs={{8,0},{12,4},{9,1},{13,5},{10,2},{14,6},{11,3},{15,7},{24,16},{28,... | collective-permute-start | bytes 393224 | tf_op jit(solution)/shard_map/ppermute | solution.py:26
  20.5 2.6 %collective-permute-start.11 = (bf16[2,256,128]{2,1,0:T(8,128)(2,1)S(1)}, bf16[2,256,128]{2,1,0:T(8,128)(2,1)S(1)}, u32[]{:S(2)}, u32[]{:S(2)}) collective-permute-start(bf16[2,256,128]{2,1,0:T(8,128)(2,1)S(1)} %get-tuple-element.55), channel_id=1, source_target_pairs={{4,0},{8,4},{12,8},{5,1},{9,5},{13,9},{6,2},{10,6},{14,10},{7,3},{... | collective-permute-start | bytes 393224 | tf_op jit(solution)/shard_map/ppermute | solution.py:26
  23.1 2.9 %collective-permute-done.refs_5_ = bf16[2,256,128]{2,1,0:T(8,128)(2,1)S(1)} collective-permute-done((bf16[2,256,128]{2,1,0:T(8,128)(2,1)S(1)}, bf16[2,256,128]{2,1,0:T(8,128)(2,1)S(1)}, u32[]{:S(2)}, u32[]{:S(2)}) %collective-permute-start) | collective-permute-done | bytes 131104 | tf_op jit(solution)/shard_map/ppermute | solution.py:26
  26.0 0.7 %collective-permute-start.9 = (bf16[2,256,128]{2,1,0:T(8,128)(2,1)S(1)}, bf16[2,256,128]{2,1,0:T(8,128)(2,1)S(1)}, u32[]{:S(2)}, u32[]{:S(2)}) collective-permute-start(bf16[2,256,128]{2,1,0:T(8,128)(2,1)S(1)} %get-tuple-element.53), channel_id=1, source_target_pairs={{12,0},{13,1},{14,2},{15,3},{28,16},{29,17},{30,18},{31,19}} | collective-permute-start | bytes 393224 | tf_op jit(solution)/shard_map/ppermute | solution.py:26
  26.6 2.3 %collective-permute-done.1.refs_6_ = bf16[2,256,128]{2,1,0:T(8,128)(2,1)S(1)} collective-permute-done((bf16[2,256,128]{2,1,0:T(8,128)(2,1)S(1)}, bf16[2,256,128]{2,1,0:T(8,128)(2,1)S(1)}, u32[]{:S(2)}, u32[]{:S(2)}) %collective-permute-start.1) | collective-permute-done | bytes 131104 | tf_op jit(solution)/shard_map/ppermute | solution.py:26
  28.9 0.0 collective-permute-done.2.refs_7_
  28.9 2.9 %shard_map.86 = (bf16[1024,128]{1,0:T(8,128)(2,1)S(1)}, bf16[1024,128]{1,0:T(8,128)(2,1)S(1)}, f32[2,256,128]{2,1,0:T(8,128)S(1)}, bf16[2,256,128]{2,1,0:T(8,128...) custom-call(s32[36]{0:T(128)S(1)} %pad_add_fusion.1.meta, ...), custom_call_target="tpu_custom_call" | custom-call | flops 1610612736 | bytes 1048576 | tf_op jit(solution)/shard_map/pallas_call | solution.py:256
  31.8 0.7 %collective-permute-start.6 = (bf16[2,256,128]{2,1,0:T(8,128)(2,1)S(1)}, bf16[2,256,128]{2,1,0:T(8,128)(2,1)S(1)}, u32[]{:S(2)}, u32[]{:S(2)}) collective-permute-start(bf16[2,256,128]{2,1,0:T(8,128)(2,1)S(1)} %get-tuple-element.49), channel_id=1, source_target_pairs={{12,0},{13,1},{14,2},{15,3},{28,16},{29,17},{30,18},{31,19}} | collective-permute-start | bytes 393224 | tf_op jit(solution)/shard_map/ppermute | solution.py:26
  32.5 1.3 %collective-permute-start.7 = (bf16[2,256,128]{2,1,0:T(8,128)(2,1)S(1)}, bf16[2,256,128]{2,1,0:T(8,128)(2,1)S(1)}, u32[]{:S(2)}, u32[]{:S(2)}) collective-permute-start(bf16[2,256,128]{2,1,0:T(8,128)(2,1)S(1)} %get-tuple-element.50), channel_id=1, source_target_pairs={{8,0},{12,4},{9,1},{13,5},{10,2},{14,6},{11,3},{15,7},{24,16},{28,... | collective-permute-start | bytes 393224 | tf_op jit(solution)/shard_map/ppermute | solution.py:26
  33.8 0.0 collective-permute-done.10
  33.8 1.9 %collective-permute-start.8 = (bf16[2,256,128]{2,1,0:T(8,128)(2,1)S(1)}, bf16[2,256,128]{2,1,0:T(8,128)(2,1)S(1)}, u32[]{:S(2)}, u32[]{:S(2)}) collective-permute-start(bf16[2,256,128]{2,1,0:T(8,128)(2,1)S(1)} %get-tuple-element.51), channel_id=1, source_target_pairs={{4,0},{8,4},{12,8},{5,1},{9,5},{13,9},{6,2},{10,6},{14,10},{7,3},{... | collective-permute-start | bytes 393224 | tf_op jit(solution)/shard_map/ppermute | solution.py:26
  35.7 0.0 collective-permute-done.11
  35.7 0.0 collective-permute-done.9
  35.8 0.1 add_convert_fusion.refs_1_
  35.8 1.1 %collective-permute-start.13 = (bf16[2,256,128]{2,1,0:T(8,128)(2,1)S(1)}, bf16[2,256,128]{2,1,0:T(8,128)(2,1)S(1)}, u32[]{:S(2)}, u32[]{:S(2)}) collective-permute-start(bf16[2,256,128]{2,1,0:T(8,128)(2,1)S(1)} %add_convert_fusion.refs_1_), channel_id=1, source_target_pairs={{0,1},{1,0},{2,3},{3,2},{4,5},{5,4},{6,7},{7,6},{8,9},{9,8},{10,11... | collective-permute-start | bytes 393224 | tf_op jit(solution)/shard_map/ppermute | solution.py:283
  36.9 0.0 collective-permute-done.6
  37.0 6.8 %collective-permute-done.7 = bf16[2,256,128]{2,1,0:T(8,128)(2,1)S(1)} collective-permute-done((bf16[2,256,128]{2,1,0:T(8,128)(2,1)S(1)}, bf16[2,256,128]{2,1,0:T(8,128)(2,1)S(1)}, u32[]{:S(2)}, u32[]{:S(2)}) %collective-permute-start.7) | collective-permute-done | bytes 131104 | tf_op jit(solution)/shard_map/ppermute | solution.py:26
  43.7 3.0 %collective-permute-done.8 = bf16[2,256,128]{2,1,0:T(8,128)(2,1)S(1)} collective-permute-done((bf16[2,256,128]{2,1,0:T(8,128)(2,1)S(1)}, bf16[2,256,128]{2,1,0:T(8,128)(2,1)S(1)}, u32[]{:S(2)}, u32[]{:S(2)}) %collective-permute-start.8) | collective-permute-done | bytes 131104 | tf_op jit(solution)/shard_map/ppermute | solution.py:26
  46.8 0.1 add_convert_fusion.1.refs_0_
  46.8 1.5 %collective-permute-start.12 = (bf16[2,256,128]{2,1,0:T(8,128)(2,1)S(1)}, bf16[2,256,128]{2,1,0:T(8,128)(2,1)S(1)}, u32[]{:S(2)}, u32[]{:S(2)}) collective-permute-start(bf16[2,256,128]{2,1,0:T(8,128)(2,1)S(1)} %add_convert_fusion.1.refs_0_), channel_id=1, source_target_pairs={{0,1},{1,0},{2,3},{3,2},{4,5},{5,4},{6,7},{7,6},{8,9},{9,8},{10,11... | collective-permute-start | bytes 393224 | tf_op jit(solution)/shard_map/ppermute | solution.py:283
  48.3 1.5 %shard_map.88 = (bf16[2048,128]{1,0:T(8,128)(2,1)}, bf16[2048,128]{1,0:T(8,128)(2,1)}) custom-call(bf16[1024,128]{1,0:T(8,128)(2,1)S(1)} %get-tuple-element.38.refs_0_, bf16[1024,128]{1,0:T(8,128)(2,1)S(1)} %get-tuple-element.39.refs_1_, bf16[1024,128]{1,0:T(8,128)(2,1)S(1)} %get-tuple-element.44.refs_2_, bf16[1024,128]{1,0:T(8,128)(2,1)S(1)} %get-tuple-element.45.refs_3_), custom_call_target="tpu_custom_call" | custom-call | bytes 1048576 | tf_op jit(solution)/shard_map/pallas_call | solution.py:277
  49.8 0.0 collective-permute-done.13.refs_3_
  49.8 0.0 collective-permute-done.12.refs_2_
  49.8 1.5 %shard_map.89 = (bf16[1024,128]{1,0:T(8,128)(2,1)}, bf16[1024,128]{1,0:T(8,128)(2,1)}) custom-call(s32[2]{0:T(128)S(1)} %pad_add_fusion.meta, bf16[2,256,128]{2,1,0:T(8,128)(2,1)S(1)} %add_convert_fusion.1.refs_0_, bf16[2,256,128]{2,1,0:T(8,128)(2,1)S(1)} %add_convert_fusion.refs_1_, bf16[2,256,128]{2,1,0:T(8,128)(2,1)S(1)} %collective-permute-done.12.refs_2_, ...), custom_call_target="tpu_custom_call" | custom-call | bytes 1048576 | tf_op jit(solution)/shard_map/pallas_call | solution.py:284
Async XLA Ops:
  0.6 12.6 %copy-start = (bf16[256,8,128]{2,1,0:T(8,128)(2,1)S(1)}, bf16[256,8,128]{2,1,0:T(8,128)(2,1)}, u32[]{:S(2)}) copy-start(bf16[256,8,128]{2,1,0:T(8,128)(2,1)} %param.5) | copy-start | bytes 1572868
  0.7 1.0 %copy-start.2 = (bf16[256,4,128]{2,1,0:T(4,128)(2,1)S(1)}, bf16[256,4,128]{2,1,0:T(4,128)(2,1)}, u32[]{:S(2)}) copy-start(bf16[256,4,128]{2,1,0:T(4,128)(2,1)} %param.6) | copy-start | bytes 786436
  1.7 0.9 %copy-start.3 = (bf16[256,4,128]{2,1,0:T(4,128)(2,1)S(1)}, bf16[256,4,128]{2,1,0:T(4,128)(2,1)}, u32[]{:S(2)}) copy-start(bf16[256,4,128]{2,1,0:T(4,128)(2,1)} %param.7) | copy-start | bytes 786436
  3.4 9.7 %copy-start.4 = (s32[2,17]{1,0:T(2,128)S(1)}, s32[2,17]{1,0:T(2,128)}, u32[]{:S(2)}) copy-start(s32[2,17]{1,0:T(2,128)} %param.9) | copy-start | bytes 412
  3.4 11.4 %collective-permute-start.3 = (bf16[2,256,128]{2,1,0:T(8,128)(2,1)S(1)}, bf16[2,256,128]{2,1,0:T(8,128)(2,1)S(1)}, u32[]{:S(2)}, u32[]{:S(2)}) collective-permute-start(bf16[2,256,128]{2,1,0:T(8,128)(2,1)S(1)} %get-tuple-element.32.refs_4_), channel_id=1, source_target_pairs={{0,4},{4,8},{8,12},{1,5},{5,9},{9,13},{2,6},{6,10},{10,14},{3,7},{... | collective-permute-start | bytes 393224 | tf_op jit(solution)/shard_map/ppermute | solution.py:26
  6.6 9.9 %collective-permute-start.4 = (bf16[2,256,128]{2,1,0:T(8,128)(2,1)S(1)}, bf16[2,256,128]{2,1,0:T(8,128)(2,1)S(1)}, u32[]{:S(2)}, u32[]{:S(2)}) collective-permute-start(bf16[2,256,128]{2,1,0:T(8,128)(2,1)S(1)} %get-tuple-element.32.refs_4_), channel_id=1, source_target_pairs={{0,8},{4,12},{1,9},{5,13},{2,10},{6,14},{3,11},{7,15},{16,24},{20,... | collective-permute-start | bytes 393224 | tf_op jit(solution)/shard_map/ppermute | solution.py:26
  8.9 7.6 %collective-permute-start.5 = (bf16[2,256,128]{2,1,0:T(8,128)(2,1)S(1)}, bf16[2,256,128]{2,1,0:T(8,128)(2,1)S(1)}, u32[]{:S(2)}, u32[]{:S(2)}) collective-permute-start(bf16[2,256,128]{2,1,0:T(8,128)(2,1)S(1)} %get-tuple-element.32.refs_4_), channel_id=1, source_target_pairs={{0,12},{1,13},{2,14},{3,15},{16,28},{17,29},{18,30},{19,31}} | collective-permute-start | bytes 393224 | tf_op jit(solution)/shard_map/ppermute | solution.py:26
  9.6 16.4 %collective-permute-start = (bf16[2,256,128]{2,1,0:T(8,128)(2,1)S(1)}, bf16[2,256,128]{2,1,0:T(8,128)(2,1)S(1)}, u32[]{:S(2)}, u32[]{:S(2)}) collective-permute-start(bf16[2,256,128]{2,1,0:T(8,128)(2,1)S(1)} %get-tuple-element.31.refs_4_), channel_id=1, source_target_pairs={{0,4},{4,8},{8,12},{1,5},{5,9},{9,13},{2,6},{6,10},{10,14},{3,7},{... | collective-permute-start | bytes 393224 | tf_op jit(solution)/shard_map/ppermute | solution.py:26
  11.8 17.1 %collective-permute-start.1 = (bf16[2,256,128]{2,1,0:T(8,128)(2,1)S(1)}, bf16[2,256,128]{2,1,0:T(8,128)(2,1)S(1)}, u32[]{:S(2)}, u32[]{:S(2)}) collective-permute-start(bf16[2,256,128]{2,1,0:T(8,128)(2,1)S(1)} %get-tuple-element.31.refs_4_), channel_id=1, source_target_pairs={{0,8},{4,12},{1,9},{5,13},{2,10},{6,14},{3,11},{7,15},{16,24},{20,... | collective-permute-start | bytes 393224 | tf_op jit(solution)/shard_map/ppermute | solution.py:26
  13.2 1.0 %copy-start.1 = (bf16[256,8,128]{2,1,0:T(8,128)(2,1)S(1)}, bf16[256,8,128]{2,1,0:T(8,128)(2,1)}, u32[]{:S(2)}) copy-start(bf16[256,8,128]{2,1,0:T(8,128)(2,1)} %param.8) | copy-start | bytes 1572868
  14.9 14.1 %collective-permute-start.2 = (bf16[2,256,128]{2,1,0:T(8,128)(2,1)S(1)}, bf16[2,256,128]{2,1,0:T(8,128)(2,1)S(1)}, u32[]{:S(2)}, u32[]{:S(2)}) collective-permute-start(bf16[2,256,128]{2,1,0:T(8,128)(2,1)S(1)} %get-tuple-element.31.refs_4_), channel_id=1, source_target_pairs={{0,12},{1,13},{2,14},{3,15},{16,28},{17,29},{18,30},{19,31}} | collective-permute-start | bytes 393224 | tf_op jit(solution)/shard_map/ppermute | solution.py:26
  19.2 14.6 %collective-permute-start.10 = (bf16[2,256,128]{2,1,0:T(8,128)(2,1)S(1)}, bf16[2,256,128]{2,1,0:T(8,128)(2,1)S(1)}, u32[]{:S(2)}, u32[]{:S(2)}) collective-permute-start(bf16[2,256,128]{2,1,0:T(8,128)(2,1)S(1)} %get-tuple-element.54), channel_id=1, source_target_pairs={{8,0},{12,4},{9,1},{13,5},{10,2},{14,6},{11,3},{15,7},{24,16},{28,... | collective-permute-start | bytes 393224 | tf_op jit(solution)/shard_map/ppermute | solution.py:26
  20.5 15.2 %collective-permute-start.11 = (bf16[2,256,128]{2,1,0:T(8,128)(2,1)S(1)}, bf16[2,256,128]{2,1,0:T(8,128)(2,1)S(1)}, u32[]{:S(2)}, u32[]{:S(2)}) collective-permute-start(bf16[2,256,128]{2,1,0:T(8,128)(2,1)S(1)} %get-tuple-element.55), channel_id=1, source_target_pairs={{4,0},{8,4},{12,8},{5,1},{9,5},{13,9},{6,2},{10,6},{14,10},{7,3},{... | collective-permute-start | bytes 393224 | tf_op jit(solution)/shard_map/ppermute | solution.py:26
  26.0 9.8 %collective-permute-start.9 = (bf16[2,256,128]{2,1,0:T(8,128)(2,1)S(1)}, bf16[2,256,128]{2,1,0:T(8,128)(2,1)S(1)}, u32[]{:S(2)}, u32[]{:S(2)}) collective-permute-start(bf16[2,256,128]{2,1,0:T(8,128)(2,1)S(1)} %get-tuple-element.53), channel_id=1, source_target_pairs={{12,0},{13,1},{14,2},{15,3},{28,16},{29,17},{30,18},{31,19}} | collective-permute-start | bytes 393224 | tf_op jit(solution)/shard_map/ppermute | solution.py:26
  31.8 5.1 %collective-permute-start.6 = (bf16[2,256,128]{2,1,0:T(8,128)(2,1)S(1)}, bf16[2,256,128]{2,1,0:T(8,128)(2,1)S(1)}, u32[]{:S(2)}, u32[]{:S(2)}) collective-permute-start(bf16[2,256,128]{2,1,0:T(8,128)(2,1)S(1)} %get-tuple-element.49), channel_id=1, source_target_pairs={{12,0},{13,1},{14,2},{15,3},{28,16},{29,17},{30,18},{31,19}} | collective-permute-start | bytes 393224 | tf_op jit(solution)/shard_map/ppermute | solution.py:26
  32.5 11.2 %collective-permute-start.7 = (bf16[2,256,128]{2,1,0:T(8,128)(2,1)S(1)}, bf16[2,256,128]{2,1,0:T(8,128)(2,1)S(1)}, u32[]{:S(2)}, u32[]{:S(2)}) collective-permute-start(bf16[2,256,128]{2,1,0:T(8,128)(2,1)S(1)} %get-tuple-element.50), channel_id=1, source_target_pairs={{8,0},{12,4},{9,1},{13,5},{10,2},{14,6},{11,3},{15,7},{24,16},{28,... | collective-permute-start | bytes 393224 | tf_op jit(solution)/shard_map/ppermute | solution.py:26
  33.8 12.9 %collective-permute-start.8 = (bf16[2,256,128]{2,1,0:T(8,128)(2,1)S(1)}, bf16[2,256,128]{2,1,0:T(8,128)(2,1)S(1)}, u32[]{:S(2)}, u32[]{:S(2)}) collective-permute-start(bf16[2,256,128]{2,1,0:T(8,128)(2,1)S(1)} %get-tuple-element.51), channel_id=1, source_target_pairs={{4,0},{8,4},{12,8},{5,1},{9,5},{13,9},{6,2},{10,6},{14,10},{7,3},{... | collective-permute-start | bytes 393224 | tf_op jit(solution)/shard_map/ppermute | solution.py:26
  35.8 13.9 %collective-permute-start.13 = (bf16[2,256,128]{2,1,0:T(8,128)(2,1)S(1)}, bf16[2,256,128]{2,1,0:T(8,128)(2,1)S(1)}, u32[]{:S(2)}, u32[]{:S(2)}) collective-permute-start(bf16[2,256,128]{2,1,0:T(8,128)(2,1)S(1)} %add_convert_fusion.refs_1_), channel_id=1, source_target_pairs={{0,1},{1,0},{2,3},{3,2},{4,5},{5,4},{6,7},{7,6},{8,9},{9,8},{10,11... | collective-permute-start | bytes 393224 | tf_op jit(solution)/shard_map/ppermute | solution.py:283
  46.8 2.9 %collective-permute-start.12 = (bf16[2,256,128]{2,1,0:T(8,128)(2,1)S(1)}, bf16[2,256,128]{2,1,0:T(8,128)(2,1)S(1)}, u32[]{:S(2)}, u32[]{:S(2)}) collective-permute-start(bf16[2,256,128]{2,1,0:T(8,128)(2,1)S(1)} %add_convert_fusion.1.refs_0_), channel_id=1, source_target_pairs={{0,1},{1,0},{2,3},{3,2},{4,5},{5,4},{6,7},{7,6},{8,9},{9,8},{10,11... | collective-permute-start | bytes 393224 | tf_op jit(solution)/shard_map/ppermute | solution.py:283

commit v3 on v2

--- a/solution.py
+++ b/solution.py
@@ -17,7 +17,6 @@
 
 VMEM = pl.BlockSpec(memory_space=pltpu.VMEM)
 SMEM = pl.BlockSpec(memory_space=pltpu.SMEM)
-HBM = pl.BlockSpec(memory_space=pltpu.HBM)
 
 
 def shifted(value, axis, steps):
@@ -32,22 +31,6 @@
 
 def dot(left, right):
     return jnp.dot(left, right, preferred_element_type=jnp.float32)
-
-
-def pack_kernel(rows, kv_heads, used, meta, key_in, value_in, *refs):
-    outs, (low, wide, sems) = (refs[:used], refs[used:])
-    copies = [
-        pltpu.make_async_copy(source, low.at[place], sems.at[place])
-        for place, source in enumerate((key_in, value_in))
-    ]
-    for copy in copies:
-        copy.start()
-    for place, copy in enumerate(copies):
-        copy.wait()
-        wide[...] = low[place].astype(jnp.float32)
-        for head in range(used):
-            picked = wide[pl.ds(meta[1] + head, rows, stride=kv_heads), :]
-            outs[head][place] = picked.astype(jnp.bfloat16)
 
 
 def turn_kernel(rows, q_heads, used, query_in, grad_in, *refs):
@@ -231,17 +214,11 @@
             cost_estimate=pl.CostEstimate(flops=flops, bytes_accessed=moved, transcendentals=0),
         )
 
-    packed = call(
-        functools.partial(pack_kernel, rows, kv_heads, used),
-        [SMEM, HBM, HBM],
-        [((2, rows, head_size), low)] * used,
-        [
-            ((2, rows * kv_heads, head_size), low),
-            ((rows * kv_heads, head_size), wide),
-            pltpu.SemaphoreType.DMA((2,)),
-        ],
-        limit=28,
-    )(meta, key_states.reshape(-1, head_size), value_states.reshape(-1, head_size))
+    packed = []
+    for head in range(used - 1, -1, -1):
+        states = [after(states, *packed[:1]) for states in (key_states, value_states)]
+        picked = [lax.dynamic_index_in_dim(heads, core_first + head, 1, keepdims=False) for heads in states]
+        packed.insert(0, jnp.stack(picked, 0))
     turned = call(
         functools.partial(turn_kernel, rows, q_heads, used),
         [VMEM, VMEM],

time: 51.7 us -> 50.5 us (0.977)
  Pallas kernels: 9.73 us -> 8.97 us
  local copies, waits for them, and re-layouts: 3.08 us -> 2.43 us
    unnamed x10 -> x12, local copies, waits for them, and re-layouts: 3 us -> 0.94 us
    dynamic_slice x0 -> x1, local copies, waits for them, and re-layouts: none -> 1.31 us  [body(): lax.dynamic_index_in_dim(heads, core_first + head, 1, keepdims=False)]
    pallas_call x1 -> x0, Pallas kernels: 0.71 us -> none  [body(): call(functools.partial(pack_kernel, rows, kv_heads, used), [SMEM, HBM, HB...]
where the time goes in v3:
time: 50.5 us; the launch traced here: 50.1 us
  starting transfers between devices  21.8 us (43%)
  waiting for transfers between devices  15.6 us (31%)
  Pallas kernels  8.97 us (18%)
  local copies, waits for them, and re-layouts  2.43 us (5%)
  between operations  0.92 us (2%)
    ppermute x12, starting transfers between devices, shifted(): lax.ppermute(value, axis, [(source, source + steps) for source in range(f...  19.2 us
    ppermute x12, waiting for transfers between devices, shifted(): lax.ppermute(value, axis, [(source, source + steps) for source in range(f...  15.6 us
    pallas_call x2, Pallas kernels, body(): call(functools.partial(attend_kernel, rows, per, lags, block_mask.shape[1...  5.49 us
    ppermute x2, starting transfers between devices, body(): others = [lax.ppermute(value, 'sub', [(0, 1), (1, 0)]) for value in sums]  2.59 us
    pallas_call x1, Pallas kernels, body(): call(functools.partial(join_kernel, rows, kv_heads, used), [SMEM] + [VMEM...  1.5 us
    pallas_call x1, Pallas kernels, body(): call(functools.partial(unturn_kernel, rows, q_heads, used), [VMEM] * (2 *...  1.47 us
    dynamic_slice x1, local copies, waits for them, and re-layouts, body(): lax.dynamic_index_in_dim(heads, core_first + head, 1, keepdims=False)  1.31 us
  transfers between devices with their start and end apart: 14, of which 5 were waited for; matrix products, arithmetic and copies ran while one was open for 1% of the time, Pallas kernels for 15%

profile of v3, /device:TPU:13, one launch (start us, length us, event | category | flops | bytes accessed | tf_op | source)
XLA Modules:
  0.0 50.1 jit_solution(6906748782191448438)
XLA Ops:
  0.7 1.3 %constant_dynamic-slice_fusion = (bf16[256,1,128]{2,1,0:T(2,128)(2,1)S(1)}, bf16[256,1,128]{2,1,0:T(2,128)(2,1)S(1)}) fusion(bf16[256,4,128]{2,1,0:T(4,128)(2,1)} %param.7, s32[]{:T(128)S(6)} %select_n.15, bf16[256,4,128]{2,1,0:T(4,128)(2,1)} %param.6), kind=kLoop, calls=%fused_computation.8 | loop fusion | bytes 262148 | tf_op jit(solution)/shard_map/jit(dynamic_index_in_dim)/dynamic_slice | solution.py:220
  2.0 0.0 copy-start.2
  2.0 3.3 %collective-permute-start.3 = (bf16[2,256,128]{2,1,0:T(8,128)(2,1)S(1)}, bf16[2,256,128]{2,1,0:T(8,128)(2,1)S(1)}, u32[]{:S(2)}, u32[]{:S(2)}) collective-permute-start(bf16[2,256,128]{2,1,0:T(8,128)(2,1)S(1)} %pad_maximum_fusion.refs_4_), channel_id=1, source_target_pairs={{0,4},{4,8},{8,12},{1,5},{5,9},{9,13},{2,6},{6,10},{10,14},{3,7},{... | collective-permute-start | bytes 393224 | tf_op jit(solution)/shard_map/ppermute | solution.py:25
  5.4 2.3 %collective-permute-start.4 = (bf16[2,256,128]{2,1,0:T(8,128)(2,1)S(1)}, bf16[2,256,128]{2,1,0:T(8,128)(2,1)S(1)}, u32[]{:S(2)}, u32[]{:S(2)}) collective-permute-start(bf16[2,256,128]{2,1,0:T(8,128)(2,1)S(1)} %pad_maximum_fusion.refs_4_), channel_id=1, source_target_pairs={{0,8},{4,12},{1,9},{5,13},{2,10},{6,14},{3,11},{7,15},{16,24},{20,... | collective-permute-start | bytes 393224 | tf_op jit(solution)/shard_map/ppermute | solution.py:25
  7.7 0.7 %collective-permute-start.5 = (bf16[2,256,128]{2,1,0:T(8,128)(2,1)S(1)}, bf16[2,256,128]{2,1,0:T(8,128)(2,1)S(1)}, u32[]{:S(2)}, u32[]{:S(2)}) collective-permute-start(bf16[2,256,128]{2,1,0:T(8,128)(2,1)S(1)} %pad_maximum_fusion.refs_4_), channel_id=1, source_target_pairs={{0,12},{1,13},{2,14},{3,15},{16,28},{17,29},{18,30},{19,31}} | collective-permute-start | bytes 393224 | tf_op jit(solution)/shard_map/ppermute | solution.py:25
  8.4 0.0 copy-done.2
  8.4 0.0 copy-start.3
  8.4 0.9 %copy-done.3 = bf16[256,4,128]{2,1,0:T(4,128)(2,1)S(1)} copy-done((bf16[256,4,128]{2,1,0:T(4,128)(2,1)S(1)}, bf16[256,4,128]{2,1,0:T(4,128)(2,1)}, u32[]{:S(2)}) %copy-start.3) | copy-done | bytes 262168
  9.3 0.0 copy-start
  9.3 0.0 copy-start.1
  9.4 0.0 copy-start.4
  9.5 2.3 %collective-permute-start = (bf16[2,256,128]{2,1,0:T(8,128)(2,1)S(1)}, bf16[2,256,128]{2,1,0:T(8,128)(2,1)S(1)}, u32[]{:S(2)}, u32[]{:S(2)}) collective-permute-start(bf16[2,256,128]{2,1,0:T(8,128)(2,1)S(1)} %pad_maximum_fusion.1.refs_4_), channel_id=1, source_target_pairs={{0,4},{4,8},{8,12},{1,5},{5,9},{9,13},{2,6},{6,10},{10,14},{3,7},{... | collective-permute-start | bytes 393224 | tf_op jit(solution)/shard_map/ppermute | solution.py:25
  11.8 1.3 %collective-permute-start.1 = (bf16[2,256,128]{2,1,0:T(8,128)(2,1)S(1)}, bf16[2,256,128]{2,1,0:T(8,128)(2,1)S(1)}, u32[]{:S(2)}, u32[]{:S(2)}) collective-permute-start(bf16[2,256,128]{2,1,0:T(8,128)(2,1)S(1)} %pad_maximum_fusion.1.refs_4_), channel_id=1, source_target_pairs={{0,8},{4,12},{1,9},{5,13},{2,10},{6,14},{3,11},{7,15},{16,24},{20,... | collective-permute-start | bytes 393224 | tf_op jit(solution)/shard_map/ppermute | solution.py:25
  13.1 0.0 copy-done.4
  13.1 0.1 reshape.33
  13.2 0.0 copy-done
  13.2 0.0 copy-done.1
  13.2 0.5 %shard_map.84 = (bf16[1024,128]{1,0:T(8,128)(2,1)S(1)}, bf16[128,1024]{1,0:T(8,128)(2,1)S(1)}, bf16[1024,128]{1,0:T(8,128)(2,1)S(1)}, bf16[128,1024]{1,0:T(8,128...) custom-call(bf16[2048,128]{1,0:T(8,128)(2,1)S(1)} %bitcast.18, ...), custom_call_target="tpu_custom_call" | custom-call | bytes 1048576 | tf_op jit(solution)/shard_map/pallas_call | solution.py:222
  13.7 0.1 pad_add_fusion.meta
  13.8 0.0 collective-permute-done.3.refs_5_
  13.8 0.7 %collective-permute-start.2 = (bf16[2,256,128]{2,1,0:T(8,128)(2,1)S(1)}, bf16[2,256,128]{2,1,0:T(8,128)(2,1)S(1)}, u32[]{:S(2)}, u32[]{:S(2)}) collective-permute-start(bf16[2,256,128]{2,1,0:T(8,128)(2,1)S(1)} %pad_maximum_fusion.1.refs_4_), channel_id=1, source_target_pairs={{0,12},{1,13},{2,14},{3,15},{16,28},{17,29},{18,30},{19,31}} | collective-permute-start | bytes 393224 | tf_op jit(solution)/shard_map/ppermute | solution.py:25
  14.5 0.9 %collective-permute-done.4.refs_6_ = bf16[2,256,128]{2,1,0:T(8,128)(2,1)S(1)} collective-permute-done((bf16[2,256,128]{2,1,0:T(8,128)(2,1)S(1)}, bf16[2,256,128]{2,1,0:T(8,128)(2,1)S(1)}, u32[]{:S(2)}, u32[]{:S(2)}) %collective-permute-start.4) | collective-permute-done | bytes 131104 | tf_op jit(solution)/shard_map/ppermute | solution.py:25
  15.3 0.0 collective-permute-done.5.refs_7_
  15.3 2.6 %shard_map.86 = (bf16[1024,128]{1,0:T(8,128)(2,1)S(1)}, bf16[1024,128]{1,0:T(8,128)(2,1)S(1)}, f32[2,256,128]{2,1,0:T(8,128)S(1)}, bf16[2,256,128]{2,1,0:T(8,128...) custom-call(s32[36]{0:T(128)S(1)} %pad_add_fusion.meta, ...), custom_call_target="tpu_custom_call" | custom-call | flops 1610612736 | bytes 1048576 | tf_op jit(solution)/shard_map/pallas_call | solution.py:233
  18.0 1.3 %collective-permute-start.10 = (bf16[2,256,128]{2,1,0:T(8,128)(2,1)S(1)}, bf16[2,256,128]{2,1,0:T(8,128)(2,1)S(1)}, u32[]{:S(2)}, u32[]{:S(2)}) collective-permute-start(bf16[2,256,128]{2,1,0:T(8,128)(2,1)S(1)} %get-tuple-element.54), channel_id=1, source_target_pairs={{8,0},{12,4},{9,1},{13,5},{10,2},{14,6},{11,3},{15,7},{24,16},{28,... | collective-permute-start | bytes 393224 | tf_op jit(solution)/shard_map/ppermute | solution.py:25
  19.3 2.8 %collective-permute-start.11 = (bf16[2,256,128]{2,1,0:T(8,128)(2,1)S(1)}, bf16[2,256,128]{2,1,0:T(8,128)(2,1)S(1)}, u32[]{:S(2)}, u32[]{:S(2)}) collective-permute-start(bf16[2,256,128]{2,1,0:T(8,128)(2,1)S(1)} %get-tuple-element.55), channel_id=1, source_target_pairs={{4,0},{8,4},{12,8},{5,1},{9,5},{13,9},{6,2},{10,6},{14,10},{7,3},{... | collective-permute-start | bytes 393224 | tf_op jit(solution)/shard_map/ppermute | solution.py:25
  22.0 2.7 %collective-permute-done.refs_5_ = bf16[2,256,128]{2,1,0:T(8,128)(2,1)S(1)} collective-permute-done((bf16[2,256,128]{2,1,0:T(8,128)(2,1)S(1)}, bf16[2,256,128]{2,1,0:T(8,128)(2,1)S(1)}, u32[]{:S(2)}, u32[]{:S(2)}) %collective-permute-start) | collective-permute-done | bytes 131104 | tf_op jit(solution)/shard_map/ppermute | solution.py:25
  24.7 0.7 %collective-permute-start.9 = (bf16[2,256,128]{2,1,0:T(8,128)(2,1)S(1)}, bf16[2,256,128]{2,1,0:T(8,128)(2,1)S(1)}, u32[]{:S(2)}, u32[]{:S(2)}) collective-permute-start(bf16[2,256,128]{2,1,0:T(8,128)(2,1)S(1)} %get-tuple-element.53), channel_id=1, source_target_pairs={{12,0},{13,1},{14,2},{15,3},{28,16},{29,17},{30,18},{31,19}} | collective-permute-start | bytes 393224 | tf_op jit(solution)/shard_map/ppermute | solution.py:25
  25.4 2.3 %collective-permute-done.1.refs_6_ = bf16[2,256,128]{2,1,0:T(8,128)(2,1)S(1)} collective-permute-done((bf16[2,256,128]{2,1,0:T(8,128)(2,1)S(1)}, bf16[2,256,128]{2,1,0:T(8,128)(2,1)S(1)}, u32[]{:S(2)}, u32[]{:S(2)}) %collective-permute-start.1) | collective-permute-done | bytes 131104 | tf_op jit(solution)/shard_map/ppermute | solution.py:25
  27.7 0.0 collective-permute-done.2.refs_7_
  27.7 2.9 %shard_map.85 = (bf16[1024,128]{1,0:T(8,128)(2,1)S(1)}, bf16[1024,128]{1,0:T(8,128)(2,1)S(1)}, f32[2,256,128]{2,1,0:T(8,128)S(1)}, bf16[2,256,128]{2,1,0:T(8,128...) custom-call(s32[36]{0:T(128)S(1)} %pad_add_fusion.meta, ...), custom_call_target="tpu_custom_call" | custom-call | flops 1610612736 | bytes 1048576 | tf_op jit(solution)/shard_map/pallas_call | solution.py:233
  30.5 0.7 %collective-permute-start.6 = (bf16[2,256,128]{2,1,0:T(8,128)(2,1)S(1)}, bf16[2,256,128]{2,1,0:T(8,128)(2,1)S(1)}, u32[]{:S(2)}, u32[]{:S(2)}) collective-permute-start(bf16[2,256,128]{2,1,0:T(8,128)(2,1)S(1)} %get-tuple-element.49), channel_id=1, source_target_pairs={{12,0},{13,1},{14,2},{15,3},{28,16},{29,17},{30,18},{31,19}} | collective-permute-start | bytes 393224 | tf_op jit(solution)/shard_map/ppermute | solution.py:25
  31.2 1.3 %collective-permute-start.7 = (bf16[2,256,128]{2,1,0:T(8,128)(2,1)S(1)}, bf16[2,256,128]{2,1,0:T(8,128)(2,1)S(1)}, u32[]{:S(2)}, u32[]{:S(2)}) collective-permute-start(bf16[2,256,128]{2,1,0:T(8,128)(2,1)S(1)} %get-tuple-element.50), channel_id=1, source_target_pairs={{8,0},{12,4},{9,1},{13,5},{10,2},{14,6},{11,3},{15,7},{24,16},{28,... | collective-permute-start | bytes 393224 | tf_op jit(solution)/shard_map/ppermute | solution.py:25
  32.5 0.0 collective-permute-done.10
  32.5 1.9 %collective-permute-start.8 = (bf16[2,256,128]{2,1,0:T(8,128)(2,1)S(1)}, bf16[2,256,128]{2,1,0:T(8,128)(2,1)S(1)}, u32[]{:S(2)}, u32[]{:S(2)}) collective-permute-start(bf16[2,256,128]{2,1,0:T(8,128)(2,1)S(1)} %get-tuple-element.51), channel_id=1, source_target_pairs={{4,0},{8,4},{12,8},{5,1},{9,5},{13,9},{6,2},{10,6},{14,10},{7,3},{... | collective-permute-start | bytes 393224 | tf_op jit(solution)/shard_map/ppermute | solution.py:25
  34.5 0.0 collective-permute-done.11
  34.5 0.0 collective-permute-done.9
  34.5 0.1 add_convert_fusion.refs_1_
  34.6 1.1 %collective-permute-start.13 = (bf16[2,256,128]{2,1,0:T(8,128)(2,1)S(1)}, bf16[2,256,128]{2,1,0:T(8,128)(2,1)S(1)}, u32[]{:S(2)}, u32[]{:S(2)}) collective-permute-start(bf16[2,256,128]{2,1,0:T(8,128)(2,1)S(1)} %add_convert_fusion.refs_1_), channel_id=1, source_target_pairs={{0,1},{1,0},{2,3},{3,2},{4,5},{5,4},{6,7},{7,6},{8,9},{9,8},{10,11... | collective-permute-start | bytes 393224 | tf_op jit(solution)/shard_map/ppermute | solution.py:260
  35.7 0.0 collective-permute-done.6
  35.7 6.8 %collective-permute-done.7 = bf16[2,256,128]{2,1,0:T(8,128)(2,1)S(1)} collective-permute-done((bf16[2,256,128]{2,1,0:T(8,128)(2,1)S(1)}, bf16[2,256,128]{2,1,0:T(8,128)(2,1)S(1)}, u32[]{:S(2)}, u32[]{:S(2)}) %collective-permute-start.7) | collective-permute-done | bytes 131104 | tf_op jit(solution)/shard_map/ppermute | solution.py:25
  42.5 3.0 %collective-permute-done.8 = bf16[2,256,128]{2,1,0:T(8,128)(2,1)S(1)} collective-permute-done((bf16[2,256,128]{2,1,0:T(8,128)(2,1)S(1)}, bf16[2,256,128]{2,1,0:T(8,128)(2,1)S(1)}, u32[]{:S(2)}, u32[]{:S(2)}) %collective-permute-start.8) | collective-permute-done | bytes 131104 | tf_op jit(solution)/shard_map/ppermute | solution.py:25
  45.5 0.1 add_convert_fusion.1.refs_0_
  45.5 1.5 %collective-permute-start.12 = (bf16[2,256,128]{2,1,0:T(8,128)(2,1)S(1)}, bf16[2,256,128]{2,1,0:T(8,128)(2,1)S(1)}, u32[]{:S(2)}, u32[]{:S(2)}) collective-permute-start(bf16[2,256,128]{2,1,0:T(8,128)(2,1)S(1)} %add_convert_fusion.1.refs_0_), channel_id=1, source_target_pairs={{0,1},{1,0},{2,3},{3,2},{4,5},{5,4},{6,7},{7,6},{8,9},{9,8},{10,11... | collective-permute-start | bytes 393224 | tf_op jit(solution)/shard_map/ppermute | solution.py:260
  47.0 0.1 pad_add_fusion.1.meta
  47.1 1.5 %shard_map.87 = (bf16[2048,128]{1,0:T(8,128)(2,1)}, bf16[2048,128]{1,0:T(8,128)(2,1)}) custom-call(bf16[1024,128]{1,0:T(8,128)(2,1)S(1)} %get-tuple-element.38.refs_0_, bf16[1024,128]{1,0:T(8,128)(2,1)S(1)} %get-tuple-element.39.refs_1_, bf16[1024,128]{1,0:T(8,128)(2,1)S(1)} %get-tuple-element.44.refs_2_, bf16[1024,128]{1,0:T(8,128)(2,1)S(1)} %get-tuple-element.45.refs_3_), custom_call_target="tpu_custom_call" | custom-call | bytes 1048576 | tf_op jit(solution)/shard_map/pallas_call | solution.py:254
  48.6 0.0 collective-permute-done.13.refs_3_
  48.6 0.0 collective-permute-done.12.refs_2_
  48.6 1.5 %shard_map.88 = (bf16[1024,128]{1,0:T(8,128)(2,1)}, bf16[1024,128]{1,0:T(8,128)(2,1)}) custom-call(s32[2]{0:T(128)S(1)} %pad_add_fusion.1.meta, bf16[2,256,128]{2,1,0:T(8,128)(2,1)S(1)} %add_convert_fusion.1.refs_0_, bf16[2,256,128]{2,1,0:T(8,128)(2,1)S(1)} %add_convert_fusion.refs_1_, bf16[2,256,128]{2,1,0:T(8,128)(2,1)S(1)} %collective-permute-done.12.refs_2_, ...), custom_call_target="tpu_custom_call" | custom-call | bytes 1048576 | tf_op jit(solution)/shard_map/pallas_call | solution.py:261
  (8 shorter events, 0.2 us)
Async XLA Ops:
  2.0 6.4 %copy-start.2 = (bf16[256,4,128]{2,1,0:T(4,128)(2,1)S(1)}, bf16[256,4,128]{2,1,0:T(4,128)(2,1)}, u32[]{:S(2)}) copy-start(bf16[256,4,128]{2,1,0:T(4,128)(2,1)} %param.6) | copy-start | bytes 786436
  2.0 11.8 %collective-permute-start.3 = (bf16[2,256,128]{2,1,0:T(8,128)(2,1)S(1)}, bf16[2,256,128]{2,1,0:T(8,128)(2,1)S(1)}, u32[]{:S(2)}, u32[]{:S(2)}) collective-permute-start(bf16[2,256,128]{2,1,0:T(8,128)(2,1)S(1)} %pad_maximum_fusion.refs_4_), channel_id=1, source_target_pairs={{0,4},{4,8},{8,12},{1,5},{5,9},{9,13},{2,6},{6,10},{10,14},{3,7},{... | collective-permute-start | bytes 393224 | tf_op jit(solution)/shard_map/ppermute | solution.py:25
  5.4 9.9 %collective-permute-start.4 = (bf16[2,256,128]{2,1,0:T(8,128)(2,1)S(1)}, bf16[2,256,128]{2,1,0:T(8,128)(2,1)S(1)}, u32[]{:S(2)}, u32[]{:S(2)}) collective-permute-start(bf16[2,256,128]{2,1,0:T(8,128)(2,1)S(1)} %pad_maximum_fusion.refs_4_), channel_id=1, source_target_pairs={{0,8},{4,12},{1,9},{5,13},{2,10},{6,14},{3,11},{7,15},{16,24},{20,... | collective-permute-start | bytes 393224 | tf_op jit(solution)/shard_map/ppermute | solution.py:25
  7.7 7.6 %collective-permute-start.5 = (bf16[2,256,128]{2,1,0:T(8,128)(2,1)S(1)}, bf16[2,256,128]{2,1,0:T(8,128)(2,1)S(1)}, u32[]{:S(2)}, u32[]{:S(2)}) collective-permute-start(bf16[2,256,128]{2,1,0:T(8,128)(2,1)S(1)} %pad_maximum_fusion.refs_4_), channel_id=1, source_target_pairs={{0,12},{1,13},{2,14},{3,15},{16,28},{17,29},{18,30},{19,31}} | collective-permute-start | bytes 393224 | tf_op jit(solution)/shard_map/ppermute | solution.py:25
  8.4 1.0 %copy-start.3 = (bf16[256,4,128]{2,1,0:T(4,128)(2,1)S(1)}, bf16[256,4,128]{2,1,0:T(4,128)(2,1)}, u32[]{:S(2)}) copy-start(bf16[256,4,128]{2,1,0:T(4,128)(2,1)} %param.7) | copy-start | bytes 786436
  9.3 3.9 %copy-start = (bf16[256,8,128]{2,1,0:T(8,128)(2,1)S(1)}, bf16[256,8,128]{2,1,0:T(8,128)(2,1)}, u32[]{:S(2)}) copy-start(bf16[256,8,128]{2,1,0:T(8,128)(2,1)} %param.5) | copy-start | bytes 1572868
  9.3 3.9 %copy-start.1 = (bf16[256,8,128]{2,1,0:T(8,128)(2,1)S(1)}, bf16[256,8,128]{2,1,0:T(8,128)(2,1)}, u32[]{:S(2)}) copy-start(bf16[256,8,128]{2,1,0:T(8,128)(2,1)} %param.8) | copy-start | bytes 1572868
  9.4 3.7 %copy-start.4 = (s32[2,17]{1,0:T(2,128)S(1)}, s32[2,17]{1,0:T(2,128)}, u32[]{:S(2)}) copy-start(s32[2,17]{1,0:T(2,128)} %param.9) | copy-start | bytes 412
  9.5 15.3 %collective-permute-start = (bf16[2,256,128]{2,1,0:T(8,128)(2,1)S(1)}, bf16[2,256,128]{2,1,0:T(8,128)(2,1)S(1)}, u32[]{:S(2)}, u32[]{:S(2)}) collective-permute-start(bf16[2,256,128]{2,1,0:T(8,128)(2,1)S(1)} %pad_maximum_fusion.1.refs_4_), channel_id=1, source_target_pairs={{0,4},{4,8},{8,12},{1,5},{5,9},{9,13},{2,6},{6,10},{10,14},{3,7},{... | collective-permute-start | bytes 393224 | tf_op jit(solution)/shard_map/ppermute | solution.py:25
  11.8 15.9 %collective-permute-start.1 = (bf16[2,256,128]{2,1,0:T(8,128)(2,1)S(1)}, bf16[2,256,128]{2,1,0:T(8,128)(2,1)S(1)}, u32[]{:S(2)}, u32[]{:S(2)}) collective-permute-start(bf16[2,256,128]{2,1,0:T(8,128)(2,1)S(1)} %pad_maximum_fusion.1.refs_4_), channel_id=1, source_target_pairs={{0,8},{4,12},{1,9},{5,13},{2,10},{6,14},{3,11},{7,15},{16,24},{20,... | collective-permute-start | bytes 393224 | tf_op jit(solution)/shard_map/ppermute | solution.py:25
  13.8 13.9 %collective-permute-start.2 = (bf16[2,256,128]{2,1,0:T(8,128)(2,1)S(1)}, bf16[2,256,128]{2,1,0:T(8,128)(2,1)S(1)}, u32[]{:S(2)}, u32[]{:S(2)}) collective-permute-start(bf16[2,256,128]{2,1,0:T(8,128)(2,1)S(1)} %pad_maximum_fusion.1.refs_4_), channel_id=1, source_target_pairs={{0,12},{1,13},{2,14},{3,15},{16,28},{17,29},{18,30},{19,31}} | collective-permute-start | bytes 393224 | tf_op jit(solution)/shard_map/ppermute | solution.py:25
  18.0 14.6 %collective-permute-start.10 = (bf16[2,256,128]{2,1,0:T(8,128)(2,1)S(1)}, bf16[2,256,128]{2,1,0:T(8,128)(2,1)S(1)}, u32[]{:S(2)}, u32[]{:S(2)}) collective-permute-start(bf16[2,256,128]{2,1,0:T(8,128)(2,1)S(1)} %get-tuple-element.54), channel_id=1, source_target_pairs={{8,0},{12,4},{9,1},{13,5},{10,2},{14,6},{11,3},{15,7},{24,16},{28,... | collective-permute-start | bytes 393224 | tf_op jit(solution)/shard_map/ppermute | solution.py:25
  19.3 15.2 %collective-permute-start.11 = (bf16[2,256,128]{2,1,0:T(8,128)(2,1)S(1)}, bf16[2,256,128]{2,1,0:T(8,128)(2,1)S(1)}, u32[]{:S(2)}, u32[]{:S(2)}) collective-permute-start(bf16[2,256,128]{2,1,0:T(8,128)(2,1)S(1)} %get-tuple-element.55), channel_id=1, source_target_pairs={{4,0},{8,4},{12,8},{5,1},{9,5},{13,9},{6,2},{10,6},{14,10},{7,3},{... | collective-permute-start | bytes 393224 | tf_op jit(solution)/shard_map/ppermute | solution.py:25
  24.7 9.7 %collective-permute-start.9 = (bf16[2,256,128]{2,1,0:T(8,128)(2,1)S(1)}, bf16[2,256,128]{2,1,0:T(8,128)(2,1)S(1)}, u32[]{:S(2)}, u32[]{:S(2)}) collective-permute-start(bf16[2,256,128]{2,1,0:T(8,128)(2,1)S(1)} %get-tuple-element.53), channel_id=1, source_target_pairs={{12,0},{13,1},{14,2},{15,3},{28,16},{29,17},{30,18},{31,19}} | collective-permute-start | bytes 393224 | tf_op jit(solution)/shard_map/ppermute | solution.py:25
  30.5 5.1 %collective-permute-start.6 = (bf16[2,256,128]{2,1,0:T(8,128)(2,1)S(1)}, bf16[2,256,128]{2,1,0:T(8,128)(2,1)S(1)}, u32[]{:S(2)}, u32[]{:S(2)}) collective-permute-start(bf16[2,256,128]{2,1,0:T(8,128)(2,1)S(1)} %get-tuple-element.49), channel_id=1, source_target_pairs={{12,0},{13,1},{14,2},{15,3},{28,16},{29,17},{30,18},{31,19}} | collective-permute-start | bytes 393224 | tf_op jit(solution)/shard_map/ppermute | solution.py:25
  31.2 11.2 %collective-permute-start.7 = (bf16[2,256,128]{2,1,0:T(8,128)(2,1)S(1)}, bf16[2,256,128]{2,1,0:T(8,128)(2,1)S(1)}, u32[]{:S(2)}, u32[]{:S(2)}) collective-permute-start(bf16[2,256,128]{2,1,0:T(8,128)(2,1)S(1)} %get-tuple-element.50), channel_id=1, source_target_pairs={{8,0},{12,4},{9,1},{13,5},{10,2},{14,6},{11,3},{15,7},{24,16},{28,... | collective-permute-start | bytes 393224 | tf_op jit(solution)/shard_map/ppermute | solution.py:25
  32.5 12.9 %collective-permute-start.8 = (bf16[2,256,128]{2,1,0:T(8,128)(2,1)S(1)}, bf16[2,256,128]{2,1,0:T(8,128)(2,1)S(1)}, u32[]{:S(2)}, u32[]{:S(2)}) collective-permute-start(bf16[2,256,128]{2,1,0:T(8,128)(2,1)S(1)} %get-tuple-element.51), channel_id=1, source_target_pairs={{4,0},{8,4},{12,8},{5,1},{9,5},{13,9},{6,2},{10,6},{14,10},{7,3},{... | collective-permute-start | bytes 393224 | tf_op jit(solution)/shard_map/ppermute | solution.py:25
  34.6 14.0 %collective-permute-start.13 = (bf16[2,256,128]{2,1,0:T(8,128)(2,1)S(1)}, bf16[2,256,128]{2,1,0:T(8,128)(2,1)S(1)}, u32[]{:S(2)}, u32[]{:S(2)}) collective-permute-start(bf16[2,256,128]{2,1,0:T(8,128)(2,1)S(1)} %add_convert_fusion.refs_1_), channel_id=1, source_target_pairs={{0,1},{1,0},{2,3},{3,2},{4,5},{5,4},{6,7},{7,6},{8,9},{9,8},{10,11... | collective-permute-start | bytes 393224 | tf_op jit(solution)/shard_map/ppermute | solution.py:260
  45.5 3.0 %collective-permute-start.12 = (bf16[2,256,128]{2,1,0:T(8,128)(2,1)S(1)}, bf16[2,256,128]{2,1,0:T(8,128)(2,1)S(1)}, u32[]{:S(2)}, u32[]{:S(2)}) collective-permute-start(bf16[2,256,128]{2,1,0:T(8,128)(2,1)S(1)} %add_convert_fusion.1.refs_0_), channel_id=1, source_target_pairs={{0,1},{1,0},{2,3},{3,2},{4,5},{5,4},{6,7},{7,6},{8,9},{9,8},{10,11... | collective-permute-start | bytes 393224 | tf_op jit(solution)/shard_map/ppermute | solution.py:260

commit v4 on v3

--- a/solution.py
+++ b/solution.py
@@ -128,9 +128,11 @@
             terms[lag - 1][1] = part.astype(jnp.bfloat16)
 
     each_lag(value_step)
-    attended_t = out_t[...].astype(jnp.bfloat16).astype(jnp.float32)
-    drift = jnp.sum(attended_t * gt_ref[...].astype(jnp.float32), axis=0, keepdims=True)
-    out_ref[...] = attended_t.T.astype(jnp.bfloat16)
+    attended_t = out_t[...].astype(jnp.bfloat16)
+    out_ref[...] = attended_t
+    drift = jnp.sum(
+        attended_t.astype(jnp.float32) * gt_ref[...].astype(jnp.float32), axis=0, keepdims=True
+    )
 
     def push_step(lag):
         for head in range(per):
@@ -150,7 +152,7 @@
             terms[lag - 1][0] = part.astype(jnp.bfloat16)
 
     each_lag(slope_step)
-    qgrad_ref[...] = (qgrad_t[...] * scale).T.astype(jnp.bfloat16)
+    qgrad_ref[...] = (qgrad_t[...] * scale).astype(jnp.bfloat16)
 
 
 def attend_kernel(rows, per, lags, offsets, meta, *refs):
@@ -169,8 +171,8 @@
     for place, target in enumerate(outs):
         for head in range(q_heads):
             slot, local = divmod(head, per)
-            tile = sources[2 * slot + place][pl.ds(local * rows, rows), :]
-            wide[pl.ds(head, rows, stride=q_heads), :] = tile.astype(jnp.float32)
+            tile = sources[2 * slot + place][:, pl.ds(local * rows, rows)]
+            wide[pl.ds(head, rows, stride=q_heads), :] = tile.astype(jnp.float32).T
         target[...] = wide[...].astype(jnp.bfloat16)
 
 
@@ -233,7 +235,7 @@
         attended, qgrad, own, *terms = call(
             functools.partial(attend_kernel, rows, per, lags, block_mask.shape[1]),
             [SMEM] + [VMEM] * (4 + lags),
-            [((width, head_size), low)] * 2
+            [((head_size, width), low)] * 2
             + [((2, rows, head_size), wide)]
             + [((2, rows, head_size), low)] * (lags - 1),
             [

time: 50.5 us -> 50.4 us (level)
  no operation moved by 1% of the time
where the time goes in v4:
time: 50.4 us; the launch traced here: 50 us
  starting transfers between devices  21.7 us (43%)
  waiting for transfers between devices  15.7 us (31%)
  Pallas kernels  8.9 us (18%)
  local copies, waits for them, and re-layouts  2.43 us (5%)
  between operations  0.92 us (2%)
    ppermute x12, starting transfers between devices, shifted(): lax.ppermute(value, axis, [(source, source + steps) for source in range(f...  19.2 us
    ppermute x12, waiting for transfers between devices, shifted(): lax.ppermute(value, axis, [(source, source + steps) for source in range(f...  15.7 us
    pallas_call x2, Pallas kernels, body(): call(functools.partial(attend_kernel, rows, per, lags, block_mask.shape[1...  5.52 us
    ppermute x2, starting transfers between devices, body(): others = [lax.ppermute(value, 'sub', [(0, 1), (1, 0)]) for value in sums]  2.57 us
    pallas_call x1, Pallas kernels, body(): call(functools.partial(join_kernel, rows, kv_heads, used), [SMEM] + [VMEM...  1.5 us
    pallas_call x1, Pallas kernels, body(): call(functools.partial(unturn_kernel, rows, q_heads, used), [VMEM] * (2 *...  1.36 us
    dynamic_slice x1, local copies, waits for them, and re-layouts, body(): lax.dynamic_index_in_dim(heads, core_first + head, 1, keepdims=False)  1.31 us
  transfers between devices with their start and end apart: 14, of which 5 were waited for; matrix products, arithmetic and copies ran while one was open for 1% of the time, Pallas kernels for 15%

profile of v4, /device:TPU:13, one launch (start us, length us, event | category | flops | bytes accessed | tf_op | source)
XLA Modules:
  0.0 50.0 jit_solution(17057986022192428289)
XLA Ops:
  0.7 1.3 %constant_dynamic-slice_fusion = (bf16[256,1,128]{2,1,0:T(2,128)(2,1)S(1)}, bf16[256,1,128]{2,1,0:T(2,128)(2,1)S(1)}) fusion(bf16[256,4,128]{2,1,0:T(4,128)(2,1)} %param.7, s32[]{:T(128)S(6)} %select_n.15, bf16[256,4,128]{2,1,0:T(4,128)(2,1)} %param.6), kind=kLoop, calls=%fused_computation.8 | loop fusion | bytes 262148 | tf_op jit(solution)/shard_map/jit(dynamic_index_in_dim)/dynamic_slice | solution.py:222
  2.0 0.0 copy-start.2
  2.0 3.3 %collective-permute-start.3 = (bf16[2,256,128]{2,1,0:T(8,128)(2,1)S(1)}, bf16[2,256,128]{2,1,0:T(8,128)(2,1)S(1)}, u32[]{:S(2)}, u32[]{:S(2)}) collective-permute-start(bf16[2,256,128]{2,1,0:T(8,128)(2,1)S(1)} %pad_maximum_fusion.refs_4_), channel_id=1, source_target_pairs={{0,4},{4,8},{8,12},{1,5},{5,9},{9,13},{2,6},{6,10},{10,14},{3,7},{... | collective-permute-start | bytes 393224 | tf_op jit(solution)/shard_map/ppermute | solution.py:25
  5.4 2.3 %collective-permute-start.4 = (bf16[2,256,128]{2,1,0:T(8,128)(2,1)S(1)}, bf16[2,256,128]{2,1,0:T(8,128)(2,1)S(1)}, u32[]{:S(2)}, u32[]{:S(2)}) collective-permute-start(bf16[2,256,128]{2,1,0:T(8,128)(2,1)S(1)} %pad_maximum_fusion.refs_4_), channel_id=1, source_target_pairs={{0,8},{4,12},{1,9},{5,13},{2,10},{6,14},{3,11},{7,15},{16,24},{20,... | collective-permute-start | bytes 393224 | tf_op jit(solution)/shard_map/ppermute | solution.py:25
  7.7 0.7 %collective-permute-start.5 = (bf16[2,256,128]{2,1,0:T(8,128)(2,1)S(1)}, bf16[2,256,128]{2,1,0:T(8,128)(2,1)S(1)}, u32[]{:S(2)}, u32[]{:S(2)}) collective-permute-start(bf16[2,256,128]{2,1,0:T(8,128)(2,1)S(1)} %pad_maximum_fusion.refs_4_), channel_id=1, source_target_pairs={{0,12},{1,13},{2,14},{3,15},{16,28},{17,29},{18,30},{19,31}} | collective-permute-start | bytes 393224 | tf_op jit(solution)/shard_map/ppermute | solution.py:25
  8.4 0.0 copy-done.2
  8.4 0.0 copy-start.3
  8.4 0.9 %copy-done.3 = bf16[256,4,128]{2,1,0:T(4,128)(2,1)S(1)} copy-done((bf16[256,4,128]{2,1,0:T(4,128)(2,1)S(1)}, bf16[256,4,128]{2,1,0:T(4,128)(2,1)}, u32[]{:S(2)}) %copy-start.3) | copy-done | bytes 262168
  9.3 0.0 copy-start
  9.3 0.0 copy-start.1
  9.4 0.0 copy-start.4
  9.5 2.3 %collective-permute-start = (bf16[2,256,128]{2,1,0:T(8,128)(2,1)S(1)}, bf16[2,256,128]{2,1,0:T(8,128)(2,1)S(1)}, u32[]{:S(2)}, u32[]{:S(2)}) collective-permute-start(bf16[2,256,128]{2,1,0:T(8,128)(2,1)S(1)} %pad_maximum_fusion.1.refs_4_), channel_id=1, source_target_pairs={{0,4},{4,8},{8,12},{1,5},{5,9},{9,13},{2,6},{6,10},{10,14},{3,7},{... | collective-permute-start | bytes 393224 | tf_op jit(solution)/shard_map/ppermute | solution.py:25
  11.8 1.3 %collective-permute-start.1 = (bf16[2,256,128]{2,1,0:T(8,128)(2,1)S(1)}, bf16[2,256,128]{2,1,0:T(8,128)(2,1)S(1)}, u32[]{:S(2)}, u32[]{:S(2)}) collective-permute-start(bf16[2,256,128]{2,1,0:T(8,128)(2,1)S(1)} %pad_maximum_fusion.1.refs_4_), channel_id=1, source_target_pairs={{0,8},{4,12},{1,9},{5,13},{2,10},{6,14},{3,11},{7,15},{16,24},{20,... | collective-permute-start | bytes 393224 | tf_op jit(solution)/shard_map/ppermute | solution.py:25
  13.1 0.0 copy-done.4
  13.1 0.1 reshape.33
  13.2 0.0 copy-done
  13.2 0.0 copy-done.1
  13.2 0.5 %shard_map.84 = (bf16[1024,128]{1,0:T(8,128)(2,1)S(1)}, bf16[128,1024]{1,0:T(8,128)(2,1)S(1)}, bf16[1024,128]{1,0:T(8,128)(2,1)S(1)}, bf16[128,1024]{1,0:T(8,128...) custom-call(bf16[2048,128]{1,0:T(8,128)(2,1)S(1)} %bitcast.18, ...), custom_call_target="tpu_custom_call" | custom-call | bytes 1048576 | tf_op jit(solution)/shard_map/pallas_call | solution.py:224
  13.7 0.1 pad_add_fusion.meta
  13.8 0.0 collective-permute-done.3.refs_5_
  13.8 0.7 %collective-permute-start.2 = (bf16[2,256,128]{2,1,0:T(8,128)(2,1)S(1)}, bf16[2,256,128]{2,1,0:T(8,128)(2,1)S(1)}, u32[]{:S(2)}, u32[]{:S(2)}) collective-permute-start(bf16[2,256,128]{2,1,0:T(8,128)(2,1)S(1)} %pad_maximum_fusion.1.refs_4_), channel_id=1, source_target_pairs={{0,12},{1,13},{2,14},{3,15},{16,28},{17,29},{18,30},{19,31}} | collective-permute-start | bytes 393224 | tf_op jit(solution)/shard_map/ppermute | solution.py:25
  14.5 0.9 %collective-permute-done.4.refs_6_ = bf16[2,256,128]{2,1,0:T(8,128)(2,1)S(1)} collective-permute-done((bf16[2,256,128]{2,1,0:T(8,128)(2,1)S(1)}, bf16[2,256,128]{2,1,0:T(8,128)(2,1)S(1)}, u32[]{:S(2)}, u32[]{:S(2)}) %collective-permute-start.4) | collective-permute-done | bytes 131104 | tf_op jit(solution)/shard_map/ppermute | solution.py:25
  15.3 0.0 collective-permute-done.5.refs_7_
  15.3 2.6 %shard_map.86 = (bf16[128,1024]{1,0:T(8,128)(2,1)S(1)}, bf16[128,1024]{1,0:T(8,128)(2,1)S(1)}, f32[2,256,128]{2,1,0:T(8,128)S(1)}, bf16[2,256,128]{2,1,0:T(8,128...) custom-call(s32[36]{0:T(128)S(1)} %pad_add_fusion.meta, ...), custom_call_target="tpu_custom_call" | custom-call | flops 1610612736 | bytes 1048576 | tf_op jit(solution)/shard_map/pallas_call | solution.py:235
  18.0 1.3 %collective-permute-start.10 = (bf16[2,256,128]{2,1,0:T(8,128)(2,1)S(1)}, bf16[2,256,128]{2,1,0:T(8,128)(2,1)S(1)}, u32[]{:S(2)}, u32[]{:S(2)}) collective-permute-start(bf16[2,256,128]{2,1,0:T(8,128)(2,1)S(1)} %get-tuple-element.54), channel_id=1, source_target_pairs={{8,0},{12,4},{9,1},{13,5},{10,2},{14,6},{11,3},{15,7},{24,16},{28,... | collective-permute-start | bytes 393224 | tf_op jit(solution)/shard_map/ppermute | solution.py:25
  19.3 2.7 %collective-permute-start.11 = (bf16[2,256,128]{2,1,0:T(8,128)(2,1)S(1)}, bf16[2,256,128]{2,1,0:T(8,128)(2,1)S(1)}, u32[]{:S(2)}, u32[]{:S(2)}) collective-permute-start(bf16[2,256,128]{2,1,0:T(8,128)(2,1)S(1)} %get-tuple-element.55), channel_id=1, source_target_pairs={{4,0},{8,4},{12,8},{5,1},{9,5},{13,9},{6,2},{10,6},{14,10},{7,3},{... | collective-permute-start | bytes 393224 | tf_op jit(solution)/shard_map/ppermute | solution.py:25
  22.0 2.7 %collective-permute-done.refs_5_ = bf16[2,256,128]{2,1,0:T(8,128)(2,1)S(1)} collective-permute-done((bf16[2,256,128]{2,1,0:T(8,128)(2,1)S(1)}, bf16[2,256,128]{2,1,0:T(8,128)(2,1)S(1)}, u32[]{:S(2)}, u32[]{:S(2)}) %collective-permute-start) | collective-permute-done | bytes 131104 | tf_op jit(solution)/shard_map/ppermute | solution.py:25
  24.7 0.7 %collective-permute-start.9 = (bf16[2,256,128]{2,1,0:T(8,128)(2,1)S(1)}, bf16[2,256,128]{2,1,0:T(8,128)(2,1)S(1)}, u32[]{:S(2)}, u32[]{:S(2)}) collective-permute-start(bf16[2,256,128]{2,1,0:T(8,128)(2,1)S(1)} %get-tuple-element.53), channel_id=1, source_target_pairs={{12,0},{13,1},{14,2},{15,3},{28,16},{29,17},{30,18},{31,19}} | collective-permute-start | bytes 393224 | tf_op jit(solution)/shard_map/ppermute | solution.py:25
  25.4 2.3 %collective-permute-done.1.refs_6_ = bf16[2,256,128]{2,1,0:T(8,128)(2,1)S(1)} collective-permute-done((bf16[2,256,128]{2,1,0:T(8,128)(2,1)S(1)}, bf16[2,256,128]{2,1,0:T(8,128)(2,1)S(1)}, u32[]{:S(2)}, u32[]{:S(2)}) %collective-permute-start.1) | collective-permute-done | bytes 131104 | tf_op jit(solution)/shard_map/ppermute | solution.py:25
  27.7 0.0 collective-permute-done.2.refs_7_
  27.7 2.9 %shard_map.85 = (bf16[128,1024]{1,0:T(8,128)(2,1)S(1)}, bf16[128,1024]{1,0:T(8,128)(2,1)S(1)}, f32[2,256,128]{2,1,0:T(8,128)S(1)}, bf16[2,256,128]{2,1,0:T(8,128...) custom-call(s32[36]{0:T(128)S(1)} %pad_add_fusion.meta, ...), custom_call_target="tpu_custom_call" | custom-call | flops 1610612736 | bytes 1048576 | tf_op jit(solution)/shard_map/pallas_call | solution.py:235
  30.6 0.7 %collective-permute-start.6 = (bf16[2,256,128]{2,1,0:T(8,128)(2,1)S(1)}, bf16[2,256,128]{2,1,0:T(8,128)(2,1)S(1)}, u32[]{:S(2)}, u32[]{:S(2)}) collective-permute-start(bf16[2,256,128]{2,1,0:T(8,128)(2,1)S(1)} %get-tuple-element.49), channel_id=1, source_target_pairs={{12,0},{13,1},{14,2},{15,3},{28,16},{29,17},{30,18},{31,19}} | collective-permute-start | bytes 393224 | tf_op jit(solution)/shard_map/ppermute | solution.py:25
  31.2 1.3 %collective-permute-start.7 = (bf16[2,256,128]{2,1,0:T(8,128)(2,1)S(1)}, bf16[2,256,128]{2,1,0:T(8,128)(2,1)S(1)}, u32[]{:S(2)}, u32[]{:S(2)}) collective-permute-start(bf16[2,256,128]{2,1,0:T(8,128)(2,1)S(1)} %get-tuple-element.50), channel_id=1, source_target_pairs={{8,0},{12,4},{9,1},{13,5},{10,2},{14,6},{11,3},{15,7},{24,16},{28,... | collective-permute-start | bytes 393224 | tf_op jit(solution)/shard_map/ppermute | solution.py:25
  32.5 0.0 collective-permute-done.10
  32.6 1.9 %collective-permute-start.8 = (bf16[2,256,128]{2,1,0:T(8,128)(2,1)S(1)}, bf16[2,256,128]{2,1,0:T(8,128)(2,1)S(1)}, u32[]{:S(2)}, u32[]{:S(2)}) collective-permute-start(bf16[2,256,128]{2,1,0:T(8,128)(2,1)S(1)} %get-tuple-element.51), channel_id=1, source_target_pairs={{4,0},{8,4},{12,8},{5,1},{9,5},{13,9},{6,2},{10,6},{14,10},{7,3},{... | collective-permute-start | bytes 393224 | tf_op jit(solution)/shard_map/ppermute | solution.py:25
  34.5 0.0 collective-permute-done.11
  34.5 0.0 collective-permute-done.9
  34.5 0.1 add_convert_fusion.refs_1_
  34.6 1.1 %collective-permute-start.13 = (bf16[2,256,128]{2,1,0:T(8,128)(2,1)S(1)}, bf16[2,256,128]{2,1,0:T(8,128)(2,1)S(1)}, u32[]{:S(2)}, u32[]{:S(2)}) collective-permute-start(bf16[2,256,128]{2,1,0:T(8,128)(2,1)S(1)} %add_convert_fusion.refs_1_), channel_id=1, source_target_pairs={{0,1},{1,0},{2,3},{3,2},{4,5},{5,4},{6,7},{7,6},{8,9},{9,8},{10,11... | collective-permute-start | bytes 393224 | tf_op jit(solution)/shard_map/ppermute | solution.py:262
  35.7 0.0 collective-permute-done.6
  35.7 6.8 %collective-permute-done.7 = bf16[2,256,128]{2,1,0:T(8,128)(2,1)S(1)} collective-permute-done((bf16[2,256,128]{2,1,0:T(8,128)(2,1)S(1)}, bf16[2,256,128]{2,1,0:T(8,128)(2,1)S(1)}, u32[]{:S(2)}, u32[]{:S(2)}) %collective-permute-start.7) | collective-permute-done | bytes 131104 | tf_op jit(solution)/shard_map/ppermute | solution.py:25
  42.5 3.0 %collective-permute-done.8 = bf16[2,256,128]{2,1,0:T(8,128)(2,1)S(1)} collective-permute-done((bf16[2,256,128]{2,1,0:T(8,128)(2,1)S(1)}, bf16[2,256,128]{2,1,0:T(8,128)(2,1)S(1)}, u32[]{:S(2)}, u32[]{:S(2)}) %collective-permute-start.8) | collective-permute-done | bytes 131104 | tf_op jit(solution)/shard_map/ppermute | solution.py:25
  45.5 0.1 add_convert_fusion.1.refs_0_
  45.6 1.5 %collective-permute-start.12 = (bf16[2,256,128]{2,1,0:T(8,128)(2,1)S(1)}, bf16[2,256,128]{2,1,0:T(8,128)(2,1)S(1)}, u32[]{:S(2)}, u32[]{:S(2)}) collective-permute-start(bf16[2,256,128]{2,1,0:T(8,128)(2,1)S(1)} %add_convert_fusion.1.refs_0_), channel_id=1, source_target_pairs={{0,1},{1,0},{2,3},{3,2},{4,5},{5,4},{6,7},{7,6},{8,9},{9,8},{10,11... | collective-permute-start | bytes 393224 | tf_op jit(solution)/shard_map/ppermute | solution.py:262
  47.0 0.1 pad_add_fusion.1.meta
  47.1 1.4 %shard_map.87 = (bf16[2048,128]{1,0:T(8,128)(2,1)}, bf16[2048,128]{1,0:T(8,128)(2,1)}) custom-call(bf16[128,1024]{1,0:T(8,128)(2,1)S(1)} %get-tuple-element.38.refs_0_, bf16[128,1024]{1,0:T(8,128)(2,1)S(1)} %get-tuple-element.39.refs_1_, bf16[128,1024]{1,0:T(8,128)(2,1)S(1)} %get-tuple-element.44.refs_2_, bf16[128,1024]{1,0:T(8,128)(2,1)S(1)} %get-tuple-element.45.refs_3_), custom_call_target="tpu_custom_call" | custom-call | bytes 1048576 | tf_op jit(solution)/shard_map/pallas_call | solution.py:256
  48.5 0.0 collective-permute-done.13.refs_3_
  48.5 0.0 collective-permute-done.12.refs_2_
  48.5 1.5 %shard_map.88 = (bf16[1024,128]{1,0:T(8,128)(2,1)}, bf16[1024,128]{1,0:T(8,128)(2,1)}) custom-call(s32[2]{0:T(128)S(1)} %pad_add_fusion.1.meta, bf16[2,256,128]{2,1,0:T(8,128)(2,1)S(1)} %add_convert_fusion.1.refs_0_, bf16[2,256,128]{2,1,0:T(8,128)(2,1)S(1)} %add_convert_fusion.refs_1_, bf16[2,256,128]{2,1,0:T(8,128)(2,1)S(1)} %collective-permute-done.12.refs_2_, ...), custom_call_target="tpu_custom_call" | custom-call | bytes 1048576 | tf_op jit(solution)/shard_map/pallas_call | solution.py:263
  (8 shorter events, 0.2 us)
Async XLA Ops:
  2.0 6.4 %copy-start.2 = (bf16[256,4,128]{2,1,0:T(4,128)(2,1)S(1)}, bf16[256,4,128]{2,1,0:T(4,128)(2,1)}, u32[]{:S(2)}) copy-start(bf16[256,4,128]{2,1,0:T(4,128)(2,1)} %param.6) | copy-start | bytes 786436
  2.0 11.8 %collective-permute-start.3 = (bf16[2,256,128]{2,1,0:T(8,128)(2,1)S(1)}, bf16[2,256,128]{2,1,0:T(8,128)(2,1)S(1)}, u32[]{:S(2)}, u32[]{:S(2)}) collective-permute-start(bf16[2,256,128]{2,1,0:T(8,128)(2,1)S(1)} %pad_maximum_fusion.refs_4_), channel_id=1, source_target_pairs={{0,4},{4,8},{8,12},{1,5},{5,9},{9,13},{2,6},{6,10},{10,14},{3,7},{... | collective-permute-start | bytes 393224 | tf_op jit(solution)/shard_map/ppermute | solution.py:25
  5.4 9.9 %collective-permute-start.4 = (bf16[2,256,128]{2,1,0:T(8,128)(2,1)S(1)}, bf16[2,256,128]{2,1,0:T(8,128)(2,1)S(1)}, u32[]{:S(2)}, u32[]{:S(2)}) collective-permute-start(bf16[2,256,128]{2,1,0:T(8,128)(2,1)S(1)} %pad_maximum_fusion.refs_4_), channel_id=1, source_target_pairs={{0,8},{4,12},{1,9},{5,13},{2,10},{6,14},{3,11},{7,15},{16,24},{20,... | collective-permute-start | bytes 393224 | tf_op jit(solution)/shard_map/ppermute | solution.py:25
  7.7 7.6 %collective-permute-start.5 = (bf16[2,256,128]{2,1,0:T(8,128)(2,1)S(1)}, bf16[2,256,128]{2,1,0:T(8,128)(2,1)S(1)}, u32[]{:S(2)}, u32[]{:S(2)}) collective-permute-start(bf16[2,256,128]{2,1,0:T(8,128)(2,1)S(1)} %pad_maximum_fusion.refs_4_), channel_id=1, source_target_pairs={{0,12},{1,13},{2,14},{3,15},{16,28},{17,29},{18,30},{19,31}} | collective-permute-start | bytes 393224 | tf_op jit(solution)/shard_map/ppermute | solution.py:25
  8.4 1.0 %copy-start.3 = (bf16[256,4,128]{2,1,0:T(4,128)(2,1)S(1)}, bf16[256,4,128]{2,1,0:T(4,128)(2,1)}, u32[]{:S(2)}) copy-start(bf16[256,4,128]{2,1,0:T(4,128)(2,1)} %param.7) | copy-start | bytes 786436
  9.3 3.9 %copy-start = (bf16[256,8,128]{2,1,0:T(8,128)(2,1)S(1)}, bf16[256,8,128]{2,1,0:T(8,128)(2,1)}, u32[]{:S(2)}) copy-start(bf16[256,8,128]{2,1,0:T(8,128)(2,1)} %param.5) | copy-start | bytes 1572868
  9.3 3.9 %copy-start.1 = (bf16[256,8,128]{2,1,0:T(8,128)(2,1)S(1)}, bf16[256,8,128]{2,1,0:T(8,128)(2,1)}, u32[]{:S(2)}) copy-start(bf16[256,8,128]{2,1,0:T(8,128)(2,1)} %param.8) | copy-start | bytes 1572868
  9.4 3.7 %copy-start.4 = (s32[2,17]{1,0:T(2,128)S(1)}, s32[2,17]{1,0:T(2,128)}, u32[]{:S(2)}) copy-start(s32[2,17]{1,0:T(2,128)} %param.9) | copy-start | bytes 412
  9.5 15.3 %collective-permute-start = (bf16[2,256,128]{2,1,0:T(8,128)(2,1)S(1)}, bf16[2,256,128]{2,1,0:T(8,128)(2,1)S(1)}, u32[]{:S(2)}, u32[]{:S(2)}) collective-permute-start(bf16[2,256,128]{2,1,0:T(8,128)(2,1)S(1)} %pad_maximum_fusion.1.refs_4_), channel_id=1, source_target_pairs={{0,4},{4,8},{8,12},{1,5},{5,9},{9,13},{2,6},{6,10},{10,14},{3,7},{... | collective-permute-start | bytes 393224 | tf_op jit(solution)/shard_map/ppermute | solution.py:25
  11.8 15.9 %collective-permute-start.1 = (bf16[2,256,128]{2,1,0:T(8,128)(2,1)S(1)}, bf16[2,256,128]{2,1,0:T(8,128)(2,1)S(1)}, u32[]{:S(2)}, u32[]{:S(2)}) collective-permute-start(bf16[2,256,128]{2,1,0:T(8,128)(2,1)S(1)} %pad_maximum_fusion.1.refs_4_), channel_id=1, source_target_pairs={{0,8},{4,12},{1,9},{5,13},{2,10},{6,14},{3,11},{7,15},{16,24},{20,... | collective-permute-start | bytes 393224 | tf_op jit(solution)/shard_map/ppermute | solution.py:25
  13.8 13.9 %collective-permute-start.2 = (bf16[2,256,128]{2,1,0:T(8,128)(2,1)S(1)}, bf16[2,256,128]{2,1,0:T(8,128)(2,1)S(1)}, u32[]{:S(2)}, u32[]{:S(2)}) collective-permute-start(bf16[2,256,128]{2,1,0:T(8,128)(2,1)S(1)} %pad_maximum_fusion.1.refs_4_), channel_id=1, source_target_pairs={{0,12},{1,13},{2,14},{3,15},{16,28},{17,29},{18,30},{19,31}} | collective-permute-start | bytes 393224 | tf_op jit(solution)/shard_map/ppermute | solution.py:25
  18.0 14.6 %collective-permute-start.10 = (bf16[2,256,128]{2,1,0:T(8,128)(2,1)S(1)}, bf16[2,256,128]{2,1,0:T(8,128)(2,1)S(1)}, u32[]{:S(2)}, u32[]{:S(2)}) collective-permute-start(bf16[2,256,128]{2,1,0:T(8,128)(2,1)S(1)} %get-tuple-element.54), channel_id=1, source_target_pairs={{8,0},{12,4},{9,1},{13,5},{10,2},{14,6},{11,3},{15,7},{24,16},{28,... | collective-permute-start | bytes 393224 | tf_op jit(solution)/shard_map/ppermute | solution.py:25
  19.3 15.2 %collective-permute-start.11 = (bf16[2,256,128]{2,1,0:T(8,128)(2,1)S(1)}, bf16[2,256,128]{2,1,0:T(8,128)(2,1)S(1)}, u32[]{:S(2)}, u32[]{:S(2)}) collective-permute-start(bf16[2,256,128]{2,1,0:T(8,128)(2,1)S(1)} %get-tuple-element.55), channel_id=1, source_target_pairs={{4,0},{8,4},{12,8},{5,1},{9,5},{13,9},{6,2},{10,6},{14,10},{7,3},{... | collective-permute-start | bytes 393224 | tf_op jit(solution)/shard_map/ppermute | solution.py:25
  24.7 9.8 %collective-permute-start.9 = (bf16[2,256,128]{2,1,0:T(8,128)(2,1)S(1)}, bf16[2,256,128]{2,1,0:T(8,128)(2,1)S(1)}, u32[]{:S(2)}, u32[]{:S(2)}) collective-permute-start(bf16[2,256,128]{2,1,0:T(8,128)(2,1)S(1)} %get-tuple-element.53), channel_id=1, source_target_pairs={{12,0},{13,1},{14,2},{15,3},{28,16},{29,17},{30,18},{31,19}} | collective-permute-start | bytes 393224 | tf_op jit(solution)/shard_map/ppermute | solution.py:25
  30.6 5.1 %collective-permute-start.6 = (bf16[2,256,128]{2,1,0:T(8,128)(2,1)S(1)}, bf16[2,256,128]{2,1,0:T(8,128)(2,1)S(1)}, u32[]{:S(2)}, u32[]{:S(2)}) collective-permute-start(bf16[2,256,128]{2,1,0:T(8,128)(2,1)S(1)} %get-tuple-element.49), channel_id=1, source_target_pairs={{12,0},{13,1},{14,2},{15,3},{28,16},{29,17},{30,18},{31,19}} | collective-permute-start | bytes 393224 | tf_op jit(solution)/shard_map/ppermute | solution.py:25
  31.2 11.2 %collective-permute-start.7 = (bf16[2,256,128]{2,1,0:T(8,128)(2,1)S(1)}, bf16[2,256,128]{2,1,0:T(8,128)(2,1)S(1)}, u32[]{:S(2)}, u32[]{:S(2)}) collective-permute-start(bf16[2,256,128]{2,1,0:T(8,128)(2,1)S(1)} %get-tuple-element.50), channel_id=1, source_target_pairs={{8,0},{12,4},{9,1},{13,5},{10,2},{14,6},{11,3},{15,7},{24,16},{28,... | collective-permute-start | bytes 393224 | tf_op jit(solution)/shard_map/ppermute | solution.py:25
  32.6 13.0 %collective-permute-start.8 = (bf16[2,256,128]{2,1,0:T(8,128)(2,1)S(1)}, bf16[2,256,128]{2,1,0:T(8,128)(2,1)S(1)}, u32[]{:S(2)}, u32[]{:S(2)}) collective-permute-start(bf16[2,256,128]{2,1,0:T(8,128)(2,1)S(1)} %get-tuple-element.51), channel_id=1, source_target_pairs={{4,0},{8,4},{12,8},{5,1},{9,5},{13,9},{6,2},{10,6},{14,10},{7,3},{... | collective-permute-start | bytes 393224 | tf_op jit(solution)/shard_map/ppermute | solution.py:25
  34.6 13.9 %collective-permute-start.13 = (bf16[2,256,128]{2,1,0:T(8,128)(2,1)S(1)}, bf16[2,256,128]{2,1,0:T(8,128)(2,1)S(1)}, u32[]{:S(2)}, u32[]{:S(2)}) collective-permute-start(bf16[2,256,128]{2,1,0:T(8,128)(2,1)S(1)} %add_convert_fusion.refs_1_), channel_id=1, source_target_pairs={{0,1},{1,0},{2,3},{3,2},{4,5},{5,4},{6,7},{7,6},{8,9},{9,8},{10,11... | collective-permute-start | bytes 393224 | tf_op jit(solution)/shard_map/ppermute | solution.py:262
  45.6 2.9 %collective-permute-start.12 = (bf16[2,256,128]{2,1,0:T(8,128)(2,1)S(1)}, bf16[2,256,128]{2,1,0:T(8,128)(2,1)S(1)}, u32[]{:S(2)}, u32[]{:S(2)}) collective-permute-start(bf16[2,256,128]{2,1,0:T(8,128)(2,1)S(1)} %add_convert_fusion.1.refs_0_), channel_id=1, source_target_pairs={{0,1},{1,0},{2,3},{3,2},{4,5},{5,4},{6,7},{7,6},{8,9},{9,8},{10,11... | collective-permute-start | bytes 393224 | tf_op jit(solution)/shard_map/ppermute | solution.py:262
